TPU v7x, 32 devices: a whole 2x2x4 slice. The times are simulated.
32 devices in a mesh: group: 8 (over y, x, core), replica: 4 (over z).
Axes of the slice: x: 2, y: 2, z: 4, core: 2. Of those that a mesh axis runs over, the one named last changes fastest.
Arguments:
- tokens: bfloat16 [4, 1024, 960], P('replica', 'group'), may hold values from -6 to 6
- positions: int32 [4, 1024], P('replica', 'group'), may hold values from 0 to 999, as said below
- gain_attn: bfloat16 [2, 960], P(None, 'group'), may hold values from 0.5 to 1.5
- w_query: bfloat16 [2, 960, 960], P(None, 'group'), may hold values from -0.1875 to 0.1875
- w_key: bfloat16 [2, 960, 320], P(None, 'group'), may hold values from -0.1875 to 0.1875
- w_value: bfloat16 [2, 960, 320], P(None, 'group'), may hold values from -0.1875 to 0.1875
- w_out: bfloat16 [2, 960, 960], P(None, 'group'), may hold values from -0.5 to 0.5
- gain_ffn: bfloat16 [2, 960], P(None, 'group'), may hold values from 0.5 to 1.5
- w_gate: bfloat16 [2, 960, 2560], P(None, 'group'), may hold values from -0.1875 to 0.1875
- w_up: bfloat16 [2, 960, 2560], P(None, 'group'), may hold values from -0.1875 to 0.1875
- w_down: bfloat16 [2, 2560, 960], P(None, 'group'), may hold values from -0.125 to 0.125
- cotangent: bfloat16 [4, 1024, 960], P('replica', 'group'), may hold values from -6 to 6
Outputs:
- activations: float32 [4, 2, 1024, 960], P('replica', None, 'group')
- grad_tokens: float32 [4, 1024, 960], P('replica', 'group')
- grad_gain_attn: float32 [2, 960], P(None, 'group')
- grad_w_query: float32 [2, 960, 960], P(None, 'group')
- grad_w_key: float32 [2, 960, 320], P(None, 'group')
- grad_w_value: float32 [2, 960, 320], P(None, 'group')
- grad_w_out: float32 [2, 960, 960], P(None, 'group')
- grad_gain_ffn: float32 [2, 960], P(None, 'group')
- grad_w_gate: float32 [2, 960, 2560], P(None, 'group')
- grad_w_up: float32 [2, 960, 2560], P(None, 'group')
- grad_w_down: float32 [2, 2560, 960], P(None, 'group')
Inputs may be any that keep to these rules, and one draw needn't show every extreme that they name: In each sequence positions are 0 at a document's first token and rise by one per token inside a document; every document except a sequence's last has 100 to 1000 tokens; the first token of every sequence has position 0.
All inputs are finite; a program needn't handle non-finite values.
Results may differ from a plain program's by a relative error of at most 0.02.
Values may be sent and summed in bfloat16 or wider, within the bound.
A program may use at most 320 MiB of HBM per device.

v0:
```python
import jax
import jax.numpy as jnp
from jax import lax
from jax.sharding import PartitionSpec as P

HEADS = 15
KV_HEADS = 5
HEAD_DIM = 64
LAYERS = 2


epsilon = 1e-05
rope_base = 100000.0


def forward_dot(left, right):
    return jnp.dot(left, right, preferred_element_type=jnp.float32)


def over_rows(left, right):
    return lax.dot_general(
        left, right, (((0,), (0,)), ((), ())), preferred_element_type=jnp.float32
    )


def against(left, right):
    return lax.dot_general(
        left, right, (((1,), (1,)), ((), ())), preferred_element_type=jnp.float32
    )


def rope_tables(token_positions):
    half_dim = HEAD_DIM // 2
    frequency = rope_base ** (-2.0 * jnp.arange(half_dim, dtype=jnp.float32) / HEAD_DIM)
    angles = token_positions.astype(jnp.float32)[:, None] * frequency[None, :]
    return (jnp.cos(angles)[:, None, :], jnp.sin(angles)[:, None, :])


def rotate(vectors, cosine, sine_table):
    half_dim = HEAD_DIM // 2
    leading, trailing = (vectors[..., :half_dim], vectors[..., half_dim:])
    return jnp.concatenate(
        [leading * cosine - trailing * sine_table, trailing * cosine + leading * sine_table],
        axis=-1,
    )


def rotate_back(vectors, cosine, sine_table):
    half_dim = HEAD_DIM // 2
    leading, trailing = (vectors[..., :half_dim], vectors[..., half_dim:])
    return jnp.concatenate(
        [leading * cosine + trailing * sine_table, trailing * cosine - leading * sine_table],
        axis=-1,
    )


def norm_forward(stream):
    inverse = lax.rsqrt(jnp.mean(stream * stream, axis=-1, keepdims=True) + epsilon)
    return (inverse, stream * inverse)


def norm_back(grad_unit, unit_value, inverse):
    return inverse * (
        grad_unit - unit_value * jnp.mean(grad_unit * unit_value, axis=-1, keepdims=True)
    )


def masked_scores(grouped, key_all, allowed):
    scores = (
        jnp.einsum("qkgd,skd->kgqs", grouped, key_all, preferred_element_type=jnp.float32) * 0.125
    )
    return jnp.where(allowed[None, None], scores, -1e30)


def layer_forward(stream, gathered, allowed, cosine, sine_table):
    gain_attn, w_query, w_key, w_value, w_out, gain_ffn, w_gate, w_up, w_down = gathered
    row_count = stream.shape[0]
    inverse_attn, unit_attn = norm_forward(stream)
    normed_attn = (unit_attn * gain_attn.astype(jnp.float32)).astype(jnp.bfloat16)
    queries = rotate(
        forward_dot(normed_attn, w_query).reshape(row_count, HEADS, HEAD_DIM), cosine, sine_table
    ).astype(jnp.bfloat16)
    own_keys = rotate(
        forward_dot(normed_attn, w_key).reshape(row_count, KV_HEADS, HEAD_DIM), cosine, sine_table
    ).astype(jnp.bfloat16)
    own_values = (
        forward_dot(normed_attn, w_value)
        .astype(jnp.bfloat16)
        .reshape(row_count, KV_HEADS, HEAD_DIM)
    )
    key_all, value_all = (
        lax.all_gather(own_keys, "group", axis=0, tiled=True),
        lax.all_gather(own_values, "group", axis=0, tiled=True),
    )
    grouped = queries.reshape(row_count, KV_HEADS, HEADS // KV_HEADS, HEAD_DIM)
    scores = masked_scores(grouped, key_all, allowed)
    row_max = jnp.max(scores, axis=-1, keepdims=True)
    exponent = jnp.exp(scores - row_max)
    row_total = jnp.sum(exponent, axis=-1, keepdims=True)
    weights_low = (exponent / row_total).astype(jnp.bfloat16)
    mixed_heads = jnp.einsum(
        "kgqs,skd->qkgd", weights_low, value_all, preferred_element_type=jnp.float32
    )
    mixed_heads = mixed_heads.reshape(row_count, HEADS * HEAD_DIM).astype(jnp.bfloat16)
    after_attn = stream + forward_dot(mixed_heads, w_out)
    inverse_ffn, unit_ffn = norm_forward(after_attn)
    normed_ffn = (unit_ffn * gain_ffn.astype(jnp.float32)).astype(jnp.bfloat16)
    gate_value = forward_dot(normed_ffn, w_gate)
    up_value = forward_dot(normed_ffn, w_up)
    hidden = (jax.nn.silu(gate_value) * up_value).astype(jnp.bfloat16)
    result = after_attn + forward_dot(hidden, w_down)
    saved = (
        unit_attn,
        inverse_attn,
        normed_attn,
        grouped,
        row_max,
        row_total,
        mixed_heads,
        unit_ffn,
        inverse_ffn,
        normed_ffn,
        gate_value,
        up_value,
        hidden,
    )
    return (result, saved, (own_keys, own_values), (key_all, value_all))


def replica_total(shares):
    (
        share_gain_attn,
        share_query,
        share_key,
        share_value,
        share_out,
        share_gain_ffn,
        share_gate,
        share_up,
        share_down,
    ) = shares
    return lax.psum(
        (
            share_gain_attn,
            share_query,
            share_key,
            share_value,
            share_out,
            share_gain_ffn,
            share_gate,
            share_up,
            share_down,
        ),
        "replica",
    )


def owned_columns(matrix, owner, members):
    width = matrix.shape[1] // members
    return lax.dynamic_slice_in_dim(matrix, owner * width, width, 1)


def layer_backward(grad_result, gathered, saved, key_all, value_all, allowed, cosine, sine_table):
    gain_attn, w_query, w_key, w_value, w_out, gain_ffn, w_gate, w_up, w_down = gathered
    (
        unit_attn,
        inverse_attn,
        normed_attn,
        grouped,
        row_max,
        row_total,
        mixed_heads,
        unit_ffn,
        inverse_ffn,
        normed_ffn,
        gate_value,
        up_value,
        hidden,
    ) = saved
    row_count = grad_result.shape[0]
    branch_low = grad_result.astype(jnp.bfloat16)
    grad_hidden = against(branch_low, w_down)
    sigmoid_gate = jax.nn.sigmoid(gate_value)
    grad_up_low = (grad_hidden * gate_value * sigmoid_gate).astype(jnp.bfloat16)
    grad_gate_low = (
        grad_hidden * up_value * sigmoid_gate * (1.0 + gate_value * (1.0 - sigmoid_gate))
    ).astype(jnp.bfloat16)
    grad_normed_ffn = against(grad_gate_low, w_gate) + against(grad_up_low, w_up)
    grad_gain_ffn = jnp.sum(grad_normed_ffn * unit_ffn, axis=0)
    grad_after = grad_result + norm_back(
        grad_normed_ffn * gain_ffn.astype(jnp.float32), unit_ffn, inverse_ffn
    )
    after_low = grad_after.astype(jnp.bfloat16)
    grad_mixed = (
        against(after_low, w_out)
        .astype(jnp.bfloat16)
        .reshape(row_count, KV_HEADS, HEADS // KV_HEADS, HEAD_DIM)
    )
    scores = masked_scores(grouped, key_all, allowed)
    weights_soft = jnp.exp(scores - row_max) / row_total
    grad_weights = jnp.einsum(
        "qkgd,skd->kgqs", grad_mixed, value_all, preferred_element_type=jnp.float32
    )
    grad_value_all = jnp.einsum(
        "kgqs,qkgd->skd",
        weights_soft.astype(jnp.bfloat16),
        grad_mixed,
        preferred_element_type=jnp.float32,
    )
    grad_scores = (
        weights_soft * (grad_weights - jnp.sum(grad_weights * weights_soft, axis=-1, keepdims=True))
    ).astype(jnp.bfloat16)
    grad_queries = (
        jnp.einsum("kgqs,skd->qkgd", grad_scores, key_all, preferred_element_type=jnp.float32)
        * 0.125
    )
    grad_key_all = (
        jnp.einsum("kgqs,qkgd->skd", grad_scores, grouped, preferred_element_type=jnp.float32)
        * 0.125
    )
    grad_keys, grad_values = (
        lax.psum_scatter(grad_key_all, "group", scatter_dimension=0, tiled=True),
        lax.psum_scatter(grad_value_all, "group", scatter_dimension=0, tiled=True),
    )
    query_back = rotate_back(grad_queries.reshape(row_count, HEADS, HEAD_DIM), cosine, sine_table)
    query_back = query_back.reshape(row_count, HEADS * HEAD_DIM).astype(jnp.bfloat16)
    key_back = (
        rotate_back(grad_keys, cosine, sine_table)
        .reshape(row_count, KV_HEADS * HEAD_DIM)
        .astype(jnp.bfloat16)
    )
    value_back = grad_values.reshape(row_count, KV_HEADS * HEAD_DIM).astype(jnp.bfloat16)
    grad_normed_attn = (
        against(query_back, w_query) + against(key_back, w_key) + against(value_back, w_value)
    )
    grad_gain_attn = jnp.sum(grad_normed_attn * unit_attn, axis=0)
    grad_stream = grad_after + norm_back(
        grad_normed_attn * gain_attn.astype(jnp.float32), unit_attn, inverse_attn
    )
    owner = lax.axis_index("group")
    members = lax.axis_size("group")
    piece_attn = lax.all_gather(normed_attn, "group", axis=0, tiled=True)
    piece_query = lax.all_gather(query_back, "group", axis=0, tiled=True)
    piece_key = lax.all_gather(key_back, "group", axis=0, tiled=True)
    piece_value = lax.all_gather(value_back, "group", axis=0, tiled=True)
    piece_mixed = lax.all_gather(mixed_heads, "group", axis=0, tiled=True)
    piece_after = lax.all_gather(after_low, "group", axis=0, tiled=True)
    piece_ffn = lax.all_gather(normed_ffn, "group", axis=0, tiled=True)
    piece_gate = lax.all_gather(grad_gate_low, "group", axis=0, tiled=True)
    piece_up = lax.all_gather(grad_up_low, "group", axis=0, tiled=True)
    piece_hidden = lax.all_gather(hidden, "group", axis=0, tiled=True)
    piece_branch = lax.all_gather(branch_low, "group", axis=0, tiled=True)
    left_attn = owned_columns(piece_attn, owner, members)
    left_mixed = owned_columns(piece_mixed, owner, members)
    left_ffn = owned_columns(piece_ffn, owner, members)
    left_hidden = owned_columns(piece_hidden, owner, members)
    gain_shares = (
        lax.psum_scatter(grad_gain_attn, "group", scatter_dimension=0, tiled=True),
        lax.psum_scatter(grad_gain_ffn, "group", scatter_dimension=0, tiled=True),
    )
    shares = (
        gain_shares[0],
        over_rows(left_attn, piece_query),
        over_rows(left_attn, piece_key),
        over_rows(left_attn, piece_value),
        over_rows(left_mixed, piece_after),
        gain_shares[1],
        over_rows(left_ffn, piece_gate),
        over_rows(left_ffn, piece_up),
        over_rows(left_hidden, piece_branch),
    )
    return (grad_stream, shares)


def on_device(
    tokens,
    positions,
    gain_attn,
    w_query,
    w_key,
    w_value,
    w_out,
    gain_ffn,
    w_gate,
    w_up,
    w_down,
    cotangent,
):
    row_count = tokens.shape[1]
    length_all = row_count * lax.axis_size("group")
    row_index = lax.axis_index("group") * row_count + jnp.arange(row_count, dtype=jnp.int32)
    token_positions = positions[0]
    key_index = jnp.arange(length_all, dtype=jnp.int32)
    allowed = (key_index[None, :] <= row_index[:, None]) & (
        key_index[None, :] >= (row_index - token_positions)[:, None]
    )
    cosine, sine_table = rope_tables(token_positions)
    stream = tokens[0].astype(jnp.float32)
    saved_all = []
    own_all = []
    full_all = []
    gathered_all = []
    outputs = []
    for layer_index in range(LAYERS):
        gathered = (
            lax.all_gather(gain_attn[layer_index], "group", axis=0, tiled=True),
            lax.all_gather(w_query[layer_index], "group", axis=0, tiled=True),
            lax.all_gather(w_key[layer_index], "group", axis=0, tiled=True),
            lax.all_gather(w_value[layer_index], "group", axis=0, tiled=True),
            lax.all_gather(w_out[layer_index], "group", axis=0, tiled=True),
            lax.all_gather(gain_ffn[layer_index], "group", axis=0, tiled=True),
            lax.all_gather(w_gate[layer_index], "group", axis=0, tiled=True),
            lax.all_gather(w_up[layer_index], "group", axis=0, tiled=True),
            lax.all_gather(w_down[layer_index], "group", axis=0, tiled=True),
        )
        stream, saved, own_pair, full_pair = layer_forward(
            stream, gathered, allowed, cosine, sine_table
        )
        saved_all.append(saved)
        own_all.append(own_pair)
        full_all.append(full_pair)
        gathered_all.append(gathered)
        outputs.append(stream)
    grad_stream = cotangent[0].astype(jnp.float32)
    owned = [None] * LAYERS
    for layer_index in reversed(range(LAYERS)):
        gathered = (
            lax.all_gather(gain_attn[layer_index], "group", axis=0, tiled=True),
            lax.all_gather(w_query[layer_index], "group", axis=0, tiled=True),
            lax.all_gather(w_key[layer_index], "group", axis=0, tiled=True),
            lax.all_gather(w_value[layer_index], "group", axis=0, tiled=True),
            lax.all_gather(w_out[layer_index], "group", axis=0, tiled=True),
            lax.all_gather(gain_ffn[layer_index], "group", axis=0, tiled=True),
            lax.all_gather(w_gate[layer_index], "group", axis=0, tiled=True),
            lax.all_gather(w_up[layer_index], "group", axis=0, tiled=True),
            lax.all_gather(w_down[layer_index], "group", axis=0, tiled=True),
        )
        key_all, value_all = (
            lax.all_gather(own_all[layer_index][0], "group", axis=0, tiled=True),
            lax.all_gather(own_all[layer_index][1], "group", axis=0, tiled=True),
        )
        grad_stream, shares = layer_backward(
            grad_stream,
            gathered,
            saved_all[layer_index],
            key_all,
            value_all,
            allowed,
            cosine,
            sine_table,
        )
        owned[layer_index] = replica_total(shares)
    stacked = tuple(
        (
            jnp.stack([owned[layer_index][member] for layer_index in range(LAYERS)])
            for member in range(9)
        )
    )
    activations = jnp.stack(outputs)[None]
    return (
        activations,
        grad_stream[None],
        stacked[0],
        stacked[1],
        stacked[2],
        stacked[3],
        stacked[4],
        stacked[5],
        stacked[6],
        stacked[7],
        stacked[8],
    )


def solution(mesh):
    in_specs = (
        P("replica", "group", None),
        P("replica", "group"),
        P(None, "group"),
        P(None, "group", None),
        P(None, "group", None),
        P(None, "group", None),
        P(None, "group", None),
        P(None, "group"),
        P(None, "group", None),
        P(None, "group", None),
        P(None, "group", None),
        P("replica", "group", None),
    )
    out_specs = (
        P("replica", None, "group", None),
        P("replica", "group", None),
        P(None, "group"),
        P(None, "group", None),
        P(None, "group", None),
        P(None, "group", None),
        P(None, "group", None),
        P(None, "group"),
        P(None, "group", None),
        P(None, "group", None),
        P(None, "group", None),
    )
    return jax.shard_map(
        on_device, mesh=mesh, in_specs=in_specs, out_specs=out_specs, check_vma=False
    )
```

profile of v0, /device:TPU:0, one launch (start us, length us, event | category | flops | bytes accessed | tf_op | source)
XLA Modules:
  0.0 1593.5 jit_solution(1129092299961670674)
XLA Ops:
  166.6 38.7 %all-gather.90.cloned.1.call-done = bf16[1,2560,960]{2,1,0:T(8,128)(2,1)} async-done(((bf16[1,320,960]{2,1,0:T(8,128)(2,1)}), bf16[1,2560,960]{2,1,0:T(8,128)(2,1)}) %all-gather.90.cloned.1.call-update) | async-done | bytes 4915216 | tf_op jit(solution)/shard_map/all_gather | solution.py:314
  271.7 39.3 %all-gather.98.cloned.1.call-done = bf16[1,960,2560]{2,1,0:T(8,128)(2,1)} async-done(((bf16[1,120,2560]{2,1,0:T(8,128)(2,1)}), bf16[1,960,2560]{2,1,0:T(8,128)(2,1)}) %all-gather.98.cloned.1.call-update) | async-done | bytes 4915216 | tf_op jit(solution)/shard_map/all_gather | solution.py:313
  315.3 39.3 %all-gather.100.cloned.1.call-done = bf16[1,2560,960]{2,1,0:T(8,128)(2,1)} async-done(((bf16[1,320,960]{2,1,0:T(8,128)(2,1)}), bf16[1,2560,960]{2,1,0:T(8,128)(2,1)}) %all-gather.100.cloned.1.call-update) | async-done | bytes 4915216 | tf_op jit(solution)/shard_map/all_gather | solution.py:314
  360.0 36.1 %all-gather.96.cloned.1.call-done = bf16[1,960,2560]{2,1,0:T(8,128)(2,1)} async-done(((bf16[1,120,2560]{2,1,0:T(8,128)(2,1)}), bf16[1,960,2560]{2,1,0:T(8,128)(2,1)}) %all-gather.96.cloned.1.call-update) | async-done | bytes 4915216 | tf_op jit(solution)/shard_map/all_gather | solution.py:312
  446.0 25.5 %reduce-scatter.5.cloned.1.call-done = f32[128,5,64]{0,2,1:T(8,128)} async-done(((f32[1024,5,64]{0,2,1:T(8,128)}), f32[128,5,64]{0,2,1:T(8,128)}) %reduce-scatter.5.cloned.1.call-update) | async-done | bytes 163856 | tf_op jit(solution)/shard_map/reduce_scatter | solution.py:222
  474.8 37.7 %reduce-scatter.7.cloned.1.call-done = f32[128,5,64]{0,2,1:T(8,128)} async-done(((f32[1024,5,64]{0,2,1:T(8,128)}), f32[128,5,64]{0,2,1:T(8,128)}) %reduce-scatter.7.cloned.1.call-update) | async-done | bytes 163856 | tf_op jit(solution)/shard_map/reduce_scatter | solution.py:223
  608.2 25.1 %all-gather.60.cloned.1.call-done = bf16[1024,960]{0,1:T(8,128)(2,1)} async-done(((bf16[128,960]{0,1:T(8,128)(2,1)}), bf16[1024,960]{0,1:T(8,128)(2,1)}) %all-gather.60.cloned.1.call-update) | async-done | bytes 1966096 | tf_op jit(solution)/shard_map/all_gather | solution.py:246
  636.5 37.8 %reduce-scatter.11.cloned.1.call-done = f32[128,5,64]{0,2,1:T(8,128)} async-done(((f32[1024,5,64]{0,2,1:T(8,128)}), f32[128,5,64]{0,2,1:T(8,128)}) %reduce-scatter.11.cloned.1.call-update) | async-done | bytes 163856 | tf_op jit(solution)/shard_map/reduce_scatter | solution.py:223
  675.2 40.1 %reduce-scatter.9.cloned.1.call-done = f32[128,5,64]{0,2,1:T(8,128)} async-done(((f32[1024,5,64]{0,2,1:T(8,128)}), f32[128,5,64]{0,2,1:T(8,128)}) %reduce-scatter.9.cloned.1.call-update) | async-done | bytes 163856 | tf_op jit(solution)/shard_map/reduce_scatter | solution.py:222
  749.0 25.8 %all-gather.50.cloned.1.call-done = bf16[1024,960]{0,1:T(8,128)(2,1)} async-done(((bf16[128,960]{0,1:T(8,128)(2,1)}), bf16[1024,960]{0,1:T(8,128)(2,1)}) %all-gather.50.cloned.1.call-update) | async-done | bytes 1966096 | tf_op jit(solution)/shard_map/all_gather | solution.py:243
  778.0 26.3 %all-gather.56.cloned.1.call-done = bf16[1024,960]{0,1:T(8,128)(2,1)} async-done(((bf16[128,960]{0,1:T(8,128)(2,1)}), bf16[1024,960]{0,1:T(8,128)(2,1)}) %all-gather.56.cloned.1.call-update) | async-done | bytes 1966096 | tf_op jit(solution)/shard_map/all_gather | solution.py:246
  804.3 30.1 %all-gather.58.cloned.1.call-done = bf16[1024,960]{0,1:T(8,128)(2,1)} async-done(((bf16[128,960]{0,1:T(8,128)(2,1)}), bf16[1024,960]{0,1:T(8,128)(2,1)}) %all-gather.58.cloned.1.call-update) | async-done | bytes 1966096 | tf_op jit(solution)/shard_map/all_gather | solution.py:247
  837.7 26.2 %all-gather.78.cloned.1.call-done = bf16[1024,960]{0,1:T(8,128)(2,1)} async-done(((bf16[128,960]{0,1:T(8,128)(2,1)}), bf16[1024,960]{0,1:T(8,128)(2,1)}) %all-gather.78.cloned.1.call-update) | async-done | bytes 1966096 | tf_op jit(solution)/shard_map/all_gather | solution.py:252
  864.0 42.9 %all-gather.76.cloned.1.call-done = bf16[1024,2560]{1,0:T(8,128)(2,1)} async-done(((bf16[128,2560]{1,0:T(8,128)(2,1)}), bf16[1024,2560]{1,0:T(8,128)(2,1)}) %all-gather.76.cloned.1.call-update) | async-done | bytes 5242896 | tf_op jit(solution)/shard_map/all_gather | solution.py:251
  911.2 25.2 %all-gather.102.cloned.1.call-done = bf16[1,1024,960]{1,2,0:T(8,128)(2,1)} async-done(((bf16[1,128,960]{1,2,0:T(8,128)(2,1)}), bf16[1,1024,960]{1,2,0:T(8,128)(2,1)}) %all-gather.102.cloned.1.call-update) | async-done | bytes 1966096 | tf_op jit(solution)/shard_map/all_gather | solution.py:252
  936.4 43.5 %all-gather.80.cloned.1.call-done = bf16[1024,2560]{1,0:T(8,128)(2,1)} async-done(((bf16[128,2560]{1,0:T(8,128)(2,1)}), bf16[1024,2560]{1,0:T(8,128)(2,1)}) %all-gather.80.cloned.1.call-update) | async-done | bytes 5242896 | tf_op jit(solution)/shard_map/all_gather | solution.py:251
  984.2 25.1 %all-gather.68.cloned.1.call-done = bf16[1024,960]{0,1:T(8,128)(2,1)} async-done(((bf16[128,960]{0,1:T(8,128)(2,1)}), bf16[1024,960]{0,1:T(8,128)(2,1)}) %all-gather.68.cloned.1.call-update) | async-done | bytes 1966096 | tf_op jit(solution)/shard_map/all_gather | solution.py:248
  1009.2 43.6 %all-gather.74.cloned.1.call-done = bf16[1024,2560]{1,0:T(8,128)(2,1)} async-done(((bf16[128,2560]{1,0:T(8,128)(2,1)}), bf16[1024,2560]{1,0:T(8,128)(2,1)}) %all-gather.74.cloned.1.call-update) | async-done | bytes 5242896 | tf_op jit(solution)/shard_map/all_gather | solution.py:250
  1057.3 39.1 %all-gather.70.cloned.1.call-done = bf16[1024,2560]{1,0:T(8,128)(2,1)} async-done(((bf16[128,2560]{1,0:T(8,128)(2,1)}), bf16[1024,2560]{1,0:T(8,128)(2,1)}) %all-gather.70.cloned.1.call-update) | async-done | bytes 5242896 | tf_op jit(solution)/shard_map/all_gather | solution.py:249
  1101.0 24.9 %all-gather.64.cloned.1.call-done = bf16[1024,960]{0,1:T(8,128)(2,1)} async-done(((bf16[128,960]{0,1:T(8,128)(2,1)}), bf16[1024,960]{0,1:T(8,128)(2,1)}) %all-gather.64.cloned.1.call-update) | async-done | bytes 1966096 | tf_op jit(solution)/shard_map/all_gather | solution.py:248
  1125.8 43.0 %all-gather.72.cloned.1.call-done = bf16[1024,2560]{1,0:T(8,128)(2,1)} async-done(((bf16[128,2560]{1,0:T(8,128)(2,1)}), bf16[1024,2560]{1,0:T(8,128)(2,1)}) %all-gather.72.cloned.1.call-update) | async-done | bytes 5242896 | tf_op jit(solution)/shard_map/all_gather | solution.py:250
  1173.5 38.4 %all-gather.66.cloned.1.call-done = bf16[1024,2560]{1,0:T(8,128)(2,1)} async-done(((bf16[128,2560]{1,0:T(8,128)(2,1)}), bf16[1024,2560]{1,0:T(8,128)(2,1)}) %all-gather.66.cloned.1.call-update) | async-done | bytes 5242896 | tf_op jit(solution)/shard_map/all_gather | solution.py:249
  1225.3 24.6 %all-reduce.8 = (f32[960]{0:T(1024)S(1)}, f32[960]{0:T(1024)S(1)}, f32[960]{0:T(1024)S(1)}, f32[960]{0:T(1024)S(1)}) all-reduce(f32[960]{0:T(1024)S(1)} %copy-done.74, f32[960]{0:T(1024)S(1)} %get-tuple-element.17, f32[960]{0:T(1024)S(1)} %copy-done.73, f32[960]{0:T(1024)S(1)} %copy-done.75), channel_id=26, replica_groups=mesh['group'=8,'replica'=4] {'group'}, use_global_device_ids=true, to_apply=%region_22.23.clone | all-reduce | flops 3840 | bytes 30720
  1264.0 311.0 %all-reduce.14.cloned.1.call-done = (f32[1,120,960]{2,1,0:T(8,128)}, f32[1,120,960]{2,1,0:T(8,128)}, f32[1,120,320]{1,2,0:T(8,128)}, f32[1,120,320]{1,2,0:T(8,12...) async-done(((f32[1,120,960]{2,1,0:T(8,128)}, ...) | async-done | bytes 9830416 | tf_op jit(solution)/shard_map/psum | solution.py:142
  (421 shorter events, 487.0 us)
Async XLA Ops:
  13.7 191.5 %all-gather.90.cloned.1.call-start = ((), (), s32[]{:S(2)}) async-start(), calls=%async_computation.29 | async-start | bytes 5898240 | tf_op jit(solution)/shard_map/all_gather | solution.py:314
  15.4 223.4 %all-gather.92.cloned.1.call-start = ((), (), s32[]{:S(2)}) async-start(), calls=%async_computation.30 | async-start | bytes 2211840 | tf_op jit(solution)/shard_map/all_gather | solution.py:307
  16.0 252.7 %all-gather.94.cloned.1.call-start = ((), (), s32[]{:S(2)}) async-start(), calls=%async_computation.31 | async-start | bytes 2211840 | tf_op jit(solution)/shard_map/all_gather | solution.py:310
  16.7 294.2 %all-gather.98.cloned.1.call-start = ((), (), s32[]{:S(2)}) async-start(), calls=%async_computation.33 | async-start | bytes 5529600 | tf_op jit(solution)/shard_map/all_gather | solution.py:313
  17.5 337.1 %all-gather.100.cloned.1.call-start = ((), (), s32[]{:S(2)}) async-start(), calls=%async_computation.34 | async-start | bytes 5898240 | tf_op jit(solution)/shard_map/all_gather | solution.py:314
  18.2 377.9 %all-gather.96.cloned.1.call-start = ((), (), s32[]{:S(2)}) async-start(), calls=%async_computation.32 | async-start | bytes 5529600 | tf_op jit(solution)/shard_map/all_gather | solution.py:312
  18.8 452.7 %reduce-scatter.5.cloned.1.call-start = ((), (), s32[]{:S(2)}) async-start(), calls=%async_computation.4 | async-start | bytes 1474560 | tf_op jit(solution)/shard_map/reduce_scatter | solution.py:222
  445.2 188.1 %all-gather.60.cloned.1.call-start = ((), (), s32[]{:S(2)}) async-start(), calls=%async_computation.14 | async-start | bytes 2211840 | tf_op jit(solution)/shard_map/all_gather | solution.py:246
  445.8 228.5 %reduce-scatter.11.cloned.1.call-start = ((), (), s32[]{:S(2)}) async-start(), calls=%async_computation.7 | async-start | bytes 1474560 | tf_op jit(solution)/shard_map/reduce_scatter | solution.py:223
  563.6 181.3 %all-gather.48.cloned.1.call-start = ((), (), s32[]{:S(2)}) async-start(), calls=%async_computation.8 | async-start | bytes 2211840 | tf_op jit(solution)/shard_map/all_gather | solution.py:242
  564.3 210.5 %all-gather.50.cloned.1.call-start = ((), (), s32[]{:S(2)}) async-start(), calls=%async_computation.9 | async-start | bytes 2211840 | tf_op jit(solution)/shard_map/all_gather | solution.py:243
  568.3 236.0 %all-gather.56.cloned.1.call-start = ((), (), s32[]{:S(2)}) async-start(), calls=%async_computation.12 | async-start | bytes 2211840 | tf_op jit(solution)/shard_map/all_gather | solution.py:246
  569.0 265.4 %all-gather.58.cloned.1.call-start = ((), (), s32[]{:S(2)}) async-start(), calls=%async_computation.13 | async-start | bytes 2211840 | tf_op jit(solution)/shard_map/all_gather | solution.py:247
  569.8 294.2 %all-gather.78.cloned.1.call-start = ((), (), s32[]{:S(2)}) async-start(), calls=%async_computation.23 | async-start | bytes 2211840 | tf_op jit(solution)/shard_map/all_gather | solution.py:252
  570.5 336.3 %all-gather.76.cloned.1.call-start = ((), (), s32[]{:S(2)}) async-start(), calls=%async_computation.22 | async-start | bytes 5898240 | tf_op jit(solution)/shard_map/all_gather | solution.py:251
  571.1 365.3 %all-gather.102.cloned.1.call-start = ((), (), s32[]{:S(2)}) async-start(), calls=%async_computation.35 | async-start | bytes 2211840 | tf_op jit(solution)/shard_map/all_gather | solution.py:252
  571.9 408.0 %all-gather.80.cloned.1.call-start = ((), (), s32[]{:S(2)}) async-start(), calls=%async_computation.24 | async-start | bytes 5898240 | tf_op jit(solution)/shard_map/all_gather | solution.py:251
  572.4 436.8 %all-gather.68.cloned.1.call-start = ((), (), s32[]{:S(2)}) async-start(), calls=%async_computation.18 | async-start | bytes 2211840 | tf_op jit(solution)/shard_map/all_gather | solution.py:248
  573.0 479.8 %all-gather.74.cloned.1.call-start = ((), (), s32[]{:S(2)}) async-start(), calls=%async_computation.21 | async-start | bytes 5898240 | tf_op jit(solution)/shard_map/all_gather | solution.py:250
  573.8 522.7 %all-gather.70.cloned.1.call-start = ((), (), s32[]{:S(2)}) async-start(), calls=%async_computation.19 | async-start | bytes 5898240 | tf_op jit(solution)/shard_map/all_gather | solution.py:249
  574.5 551.3 %all-gather.64.cloned.1.call-start = ((), (), s32[]{:S(2)}) async-start(), calls=%async_computation.16 | async-start | bytes 2211840 | tf_op jit(solution)/shard_map/all_gather | solution.py:248
  575.1 593.8 %all-gather.72.cloned.1.call-start = ((), (), s32[]{:S(2)}) async-start(), calls=%async_computation.20 | async-start | bytes 5898240 | tf_op jit(solution)/shard_map/all_gather | solution.py:250
  575.8 636.1 %all-gather.66.cloned.1.call-start = ((), (), s32[]{:S(2)}) async-start(), calls=%async_computation.17 | async-start | bytes 5898240 | tf_op jit(solution)/shard_map/all_gather | solution.py:249
  576.6 998.4 %all-reduce.14.cloned.1.call-start = ((), (), s32[]{:S(2)}) async-start(), calls=%async_computation.36 | async-start | bytes 20316160 | tf_op jit(solution)/shard_map/psum | solution.py:142
  (105 other events, 2377.1 us)
Sparse Core Ops, SparseCore 0:
  10.5 30.1 all-gather.81
  72.4 47.8 all-gather.85
  122.0 39.7 all-gather.87
  164.1 41.1 all-gather.89
  207.5 31.2 all-gather.91
  271.2 39.7 all-gather.97
  313.4 41.1 all-gather.99
  356.3 39.7 all-gather.95
  434.1 37.3 reduce-scatter.4
  475.2 37.3 reduce-scatter.6
  544.4 27.6 all-gather.53
  573.7 30.1 all-gather.61
  636.9 37.3 reduce-scatter.10
  678.0 37.3 reduce-scatter.8
  747.1 27.6 all-gather.49
  776.7 27.6 all-gather.55
  865.7 41.1 all-gather.75
  908.7 27.6 all-gather.101
  938.7 41.1 all-gather.79
  1011.7 41.1 all-gather.73
  1055.3 41.1 all-gather.69
  1127.7 41.1 all-gather.71
  1170.7 41.1 all-gather.65
  1217.5 357.5 all-reduce.13
  (9 shorter events, 247.4 us)
where the time goes:
time: 1600 us; the launch traced here: 1590 us
  waiting for transfers between devices  1100 us (69%)
  blocking collectives  205 us (13%)
  matrix products  191 us (12%)
  other arithmetic  38.1 us (2%)
  local copies, waits for them, and re-layouts  36.4 us (2%)
  between operations  17.4 us (1%)
    psum x1, waiting for transfers between devices, replica_total(): lax.psum((share_gain_attn, share_query, share_key, share_value, share_out...  311 us
    all_gather x2, waiting for transfers between devices, layer_backward(): piece_up = lax.all_gather(grad_up_low, 'group', axis=0, tiled=True)  86.6 us
    all_gather x2, waiting for transfers between devices, layer_backward(): piece_hidden = lax.all_gather(hidden, 'group', axis=0, tiled=True)  86.4 us
    all_gather x2, waiting for transfers between devices, on_device(): lax.all_gather(w_down[layer_index], 'group', axis=0, tiled=True)  78 us
    all_gather x2, waiting for transfers between devices, layer_backward(): piece_gate = lax.all_gather(grad_gate_low, 'group', axis=0, tiled=True)  77.5 us
    reduce_scatter x2, waiting for transfers between devices, layer_backward(): lax.psum_scatter(grad_value_all, 'group', scatter_dimension=0, tiled=True)  75.5 us
    reduce_scatter x2, waiting for transfers between devices, layer_backward(): lax.psum_scatter(grad_key_all, 'group', scatter_dimension=0, tiled=True)  65.6 us
    all_gather x2, waiting for transfers between devices, layer_backward(): piece_branch = lax.all_gather(branch_low, 'group', axis=0, tiled=True)  51.5 us
  transfers between devices with their start and end apart: 33, of which 27 were waited for; matrix products, arithmetic and copies ran while one was open for 13% of the time, Pallas kernels for 0%

commit v1 on v0

v1 whole, which is shorter than its diff:
```python
import jax
import jax.numpy as jnp
from jax import lax
from jax.experimental import pallas as pl
from jax.experimental.pallas import tpu as pltpu
from jax.sharding import PartitionSpec as P

HEADS = 15
KV_HEADS = 5
HEAD_DIM = 64
LAYERS = 2
SHARE = HEADS // KV_HEADS

epsilon = 1e-05
rope_base = 100000.0
low = jnp.bfloat16


def dot(left, right):
    return jnp.dot(left, right, preferred_element_type=jnp.float32)


def over_rows(left, right):
    return lax.dot_general(
        left, right, (((0,), (0,)), ((), ())), preferred_element_type=jnp.float32
    )


def against(left, right):
    return lax.dot_general(
        left, right, (((1,), (1,)), ((), ())), preferred_element_type=jnp.float32
    )


def gather_kernel(members, block_ref, out_ref, local_sem, send_sem, recv_sem, pass_sem, got_sem):
    me = lax.axis_index("group")
    chips = members // 2
    chip, core = lax.div(me, 2), lax.rem(me, 2)
    sibling = chip * 2 + 1 - core
    barrier = pltpu.get_barrier_semaphore()
    pl.semaphore_signal(barrier, inc=1, device_id={"group": sibling})
    for step in range(1, chips):
        peer = lax.rem(chip + step, chips) * 2 + core
        pl.semaphore_signal(barrier, inc=1, device_id={"group": peer})
    pl.semaphore_wait(barrier, chips)
    sends = []
    for step in range(1, chips):
        peer = lax.rem(chip + step, chips) * 2 + core
        copy = pltpu.make_async_remote_copy(
            src_ref=block_ref,
            dst_ref=out_ref.at[me],
            send_sem=send_sem.at[step],
            recv_sem=recv_sem.at[step],
            device_id={"group": peer},
        )
        copy.start()
        sends.append(copy)
    own = pltpu.make_async_remote_copy(
        src_ref=block_ref,
        dst_ref=out_ref.at[me],
        send_sem=pass_sem.at[0],
        recv_sem=got_sem.at[0],
        device_id={"group": sibling},
    )
    own.start()
    local = pltpu.make_async_copy(block_ref, out_ref.at[me], local_sem)
    local.start()
    passes = [own]
    for step in range(1, chips):
        sends[step - 1].wait_recv()
        source = lax.rem(chip - step + chips, chips) * 2 + core
        copy = pltpu.make_async_remote_copy(
            src_ref=out_ref.at[source],
            dst_ref=out_ref.at[source],
            send_sem=pass_sem.at[step],
            recv_sem=got_sem.at[step],
            device_id={"group": sibling},
        )
        copy.start()
        passes.append(copy)
    local.wait()
    for copy in passes:
        copy.wait()
    for copy in sends:
        copy.wait_send()


def gather(block, members):
    rows, width = block.shape
    out = pl.pallas_call(
        lambda *refs: gather_kernel(members, *refs),
        out_shape=jax.ShapeDtypeStruct((members, rows, width), block.dtype),
        in_specs=[pl.BlockSpec(memory_space=pltpu.VMEM)],
        out_specs=pl.BlockSpec(memory_space=pltpu.VMEM),
        scratch_shapes=[pltpu.SemaphoreType.DMA]
        + [pltpu.SemaphoreType.DMA((members // 2,)) for _ in range(4)],
        compiler_params=pltpu.CompilerParams(
            collective_id=0, has_side_effects=True, vmem_limit_bytes=24 * 2**20
        ),
        cost_estimate=pl.CostEstimate(
            flops=0, bytes_accessed=30_000_000, transcendentals=0
        ),
    )(block)
    return out.reshape(members * rows, width)


def scatter_kernel(
    members, part_ref, out_ref, pair_ref, ready_ref, land_ref, pair_send, pair_recv, send_sem, recv_sem
):
    me = lax.axis_index("group")
    chips = members // 2
    chip, core = lax.div(me, 2), lax.rem(me, 2)
    sibling = chip * 2 + 1 - core
    barrier = pltpu.get_barrier_semaphore()
    pl.semaphore_signal(barrier, inc=1, device_id={"group": sibling})
    for step in range(1, chips):
        peer = lax.rem(chip + step, chips) * 2 + core
        pl.semaphore_signal(barrier, inc=1, device_id={"group": peer})
    pl.semaphore_wait(barrier, chips)
    pairs = []
    for step in range(chips):
        place = lax.rem(chip + step + 1, chips)
        copy = pltpu.make_async_remote_copy(
            src_ref=part_ref.at[place * 2 + 1 - core],
            dst_ref=pair_ref.at[step],
            send_sem=pair_send.at[step],
            recv_sem=pair_recv.at[step],
            device_id={"group": sibling},
        )
        copy.start()
        pairs.append(copy)
    sends = []
    for step in range(chips):
        place = lax.rem(chip + step + 1, chips)
        pairs[step].wait_recv()
        total = part_ref[place * 2 + core].astype(jnp.float32) + pair_ref[step].astype(jnp.float32)
        if step == chips - 1:
            out_ref[...] = total
            break
        ready_ref[step] = total.astype(low)
        copy = pltpu.make_async_remote_copy(
            src_ref=ready_ref.at[step],
            dst_ref=land_ref.at[step],
            send_sem=send_sem.at[step],
            recv_sem=recv_sem.at[step],
            device_id={"group": place * 2 + core},
        )
        copy.start()
        sends.append(copy)
    for step in range(chips - 1):
        sends[step].wait_recv()
        out_ref[...] += land_ref[step].astype(jnp.float32)
    for copy in pairs + sends:
        copy.wait_send()


def scatter_sum(partial, members):
    length, width = partial.shape
    rows = length // members
    chips = members // 2
    return pl.pallas_call(
        lambda *refs: scatter_kernel(members, *refs),
        out_shape=jax.ShapeDtypeStruct((rows, width), jnp.float32),
        in_specs=[pl.BlockSpec(memory_space=pltpu.VMEM)],
        out_specs=pl.BlockSpec(memory_space=pltpu.VMEM),
        scratch_shapes=[
            pltpu.VMEM((chips, rows, width), low),
            pltpu.VMEM((chips, rows, width), low),
            pltpu.VMEM((chips, rows, width), low),
        ]
        + [pltpu.SemaphoreType.DMA((chips,)) for _ in range(4)],
        compiler_params=pltpu.CompilerParams(
            collective_id=1, has_side_effects=True, vmem_limit_bytes=24 * 2**20
        ),
        cost_estimate=pl.CostEstimate(
            flops=0, bytes_accessed=30_000_000, transcendentals=0
        ),
    )(partial.astype(low).reshape(members, rows, width))


def swap(blocks):
    return lax.all_to_all(blocks, "group", split_axis=0, concat_axis=0, tiled=True)


def rope_tables(token_positions):
    half_dim = HEAD_DIM // 2
    frequency = rope_base ** (-2.0 * jnp.arange(half_dim, dtype=jnp.float32) / HEAD_DIM)
    angles = token_positions.astype(jnp.float32)[:, None] * frequency[None, :]
    return (jnp.cos(angles)[:, None, :], jnp.sin(angles)[:, None, :])


def rotate(vectors, cosine, sine_table):
    half_dim = HEAD_DIM // 2
    leading, trailing = (vectors[..., :half_dim], vectors[..., half_dim:])
    return jnp.concatenate(
        [leading * cosine - trailing * sine_table, trailing * cosine + leading * sine_table],
        axis=-1,
    )


def norm_forward(stream):
    inverse = lax.rsqrt(jnp.mean(stream * stream, axis=-1, keepdims=True) + epsilon)
    return (inverse, stream * inverse)


def norm_back(grad_unit, unit_value, inverse):
    return inverse * (
        grad_unit - unit_value * jnp.mean(grad_unit * unit_value, axis=-1, keepdims=True)
    )


def pad_columns(matrix, width):
    return jnp.pad(matrix, ((0, 0), (0, width - matrix.shape[1])))


def widen(matrix):
    rows = matrix.shape[0]
    wide = matrix.reshape(rows, KV_HEADS, 1, HEAD_DIM)
    wide = jnp.broadcast_to(wide, (rows, KV_HEADS, SHARE, HEAD_DIM))
    return wide.reshape(rows, HEADS * HEAD_DIM)


def by_member(matrix, members):
    rows, width = matrix.shape
    return matrix.reshape(rows, members, width // members).transpose(1, 0, 2)


def by_row(blocks):
    members, rows, width = blocks.shape
    return blocks.transpose(1, 0, 2).reshape(rows, members * width)


def on_device(
    tokens,
    positions,
    gain_attn,
    w_query,
    w_key,
    w_value,
    w_out,
    gain_ffn,
    w_gate,
    w_up,
    w_down,
    cotangent,
):
    row_count = tokens.shape[1]
    members = lax.axis_size("group")
    owner = lax.axis_index("group")
    length = row_count * members
    own_rows = w_query.shape[1]
    width = own_rows * members
    local_heads = -(-HEADS // members)
    span = local_heads * HEAD_DIM
    padded = span * members
    part_ff = w_gate.shape[2] // members

    all_positions = lax.all_gather(positions[0], "group", axis=0, tiled=True)
    gains = lax.all_gather(
        jnp.concatenate([gain_attn, gain_ffn], axis=0), "group", axis=1, tiled=True
    ).astype(jnp.float32)

    weights = []
    for layer in range(LAYERS):
        attn_blocks = jnp.concatenate(
            [
                by_member(pad_columns(w_query[layer], padded), members),
                by_member(pad_columns(widen(w_key[layer]), padded), members),
                by_member(pad_columns(widen(w_value[layer]), padded), members),
            ],
            axis=2,
        )
        ffn_blocks = jnp.concatenate(
            [by_member(w_gate[layer], members), by_member(w_up[layer], members)], axis=2
        )
        attn_weight = swap(attn_blocks).reshape(width, 3 * span)
        ffn_weight = swap(ffn_blocks).reshape(width, 2 * part_ff)
        weights.append([attn_weight, ffn_weight])
    next_out = lax.ppermute(
        w_out, "group", [(member, member - 1) for member in range(1, members)]
    )
    slab = jnp.concatenate(
        [w_out, next_out, jnp.zeros((LAYERS, span - own_rows, width), w_out.dtype)], axis=1
    )
    out_all = lax.dynamic_slice_in_dim(slab, owner * (span - own_rows), span, 1)

    token_index = jnp.arange(length, dtype=jnp.int32)
    allowed = (token_index[None, :] <= token_index[:, None]) & (
        token_index[None, :] >= (token_index - all_positions)[:, None]
    )
    cosine, sine_table = rope_tables(all_positions)

    def heads_of(matrix):
        return matrix.reshape(length, local_heads, HEAD_DIM)

    stream = tokens[0].astype(jnp.float32)
    saved_all = []
    outputs = []
    for layer in range(LAYERS):
        attn_weight, ffn_weight = weights[layer]
        inverse_attn, unit_attn = norm_forward(stream)
        normed_attn = gather((unit_attn * gains[layer]).astype(low), members)
        product = dot(normed_attn, attn_weight)
        queries = rotate(heads_of(product[:, :span]), cosine, sine_table).astype(low)
        keys = rotate(heads_of(product[:, span : 2 * span]), cosine, sine_table).astype(low)
        values = heads_of(product[:, 2 * span :]).astype(low)
        scores = (
            jnp.einsum("thd,shd->hts", queries, keys, preferred_element_type=jnp.float32) * 0.125
        )
        scores = jnp.where(allowed[None], scores, -1e30)
        exponent = jnp.exp(scores - jnp.max(scores, axis=-1, keepdims=True))
        probs = (exponent / jnp.sum(exponent, axis=-1, keepdims=True)).astype(low)
        mixed = jnp.einsum("hts,shd->thd", probs, values, preferred_element_type=jnp.float32)
        mixed = mixed.reshape(length, span).astype(low)
        after = stream + scatter_sum(dot(mixed, out_all[layer]), members)
        inverse_ffn, unit_ffn = norm_forward(after)
        normed_ffn = gather((unit_ffn * gains[LAYERS + layer]).astype(low), members)
        both = dot(normed_ffn, ffn_weight)
        gate, up = both[:, :part_ff], both[:, part_ff:]
        hidden = (jax.nn.silu(gate) * up).astype(low)
        stream = after + scatter_sum(dot(hidden, w_down[layer]), members)
        outputs.append(stream)
        saved_all.append(
            (
                inverse_attn, unit_attn, normed_attn, queries, keys, values, probs, mixed,
                inverse_ffn, unit_ffn, normed_ffn, gate, up, hidden,
            )
        )

    grad_result = cotangent[0].astype(jnp.float32)
    owned = [None] * LAYERS
    gain_sums = [None] * (2 * LAYERS)
    for layer in reversed(range(LAYERS)):
        attn_weight, ffn_weight = weights[layer]
        (
            inverse_attn, unit_attn, normed_attn, queries, keys, values, probs, mixed,
            inverse_ffn, unit_ffn, normed_ffn, gate, up, hidden,
        ) = saved_all[layer]
        out_low = gather(grad_result.astype(low), members)
        grad_hidden = against(out_low, w_down[layer])
        sigmoid = jax.nn.sigmoid(gate)
        grad_up = (grad_hidden * gate * sigmoid).astype(low)
        grad_gate = (grad_hidden * up * sigmoid * (1.0 + gate * (1.0 - sigmoid))).astype(low)
        grad_both = jnp.concatenate([grad_gate, grad_up], axis=1)
        grad_normed_ffn = scatter_sum(against(grad_both, ffn_weight), members)
        grad_down = over_rows(hidden, out_low).astype(low)
        grad_ffn_weight = swap(
            over_rows(normed_ffn, grad_both).astype(low).reshape(members, own_rows, 2 * part_ff)
        )
        gain_sums[LAYERS + layer] = jnp.sum(grad_normed_ffn * unit_ffn, axis=0)
        grad_after = grad_result + norm_back(
            grad_normed_ffn * gains[LAYERS + layer], unit_ffn, inverse_ffn
        )
        after_low = gather(grad_after.astype(low), members)
        grad_mixed = against(after_low, out_all[layer]).astype(low)
        grad_out = over_rows(mixed, after_low).astype(low)
        delta = jnp.sum(
            heads_of(grad_mixed.astype(jnp.float32) * mixed.astype(jnp.float32)), axis=-1
        ).T[:, :, None]
        grad_heads = heads_of(grad_mixed)
        grad_probs = jnp.einsum(
            "thd,shd->hts", grad_heads, values, preferred_element_type=jnp.float32
        )
        grad_values = jnp.einsum(
            "hts,thd->shd", probs, grad_heads, preferred_element_type=jnp.float32
        )
        grad_scores = (probs.astype(jnp.float32) * (grad_probs - delta)).astype(low)
        grad_queries = 0.125 * jnp.einsum(
            "hts,shd->thd", grad_scores, keys, preferred_element_type=jnp.float32
        )
        grad_keys = 0.125 * jnp.einsum(
            "hts,thd->shd", grad_scores, queries, preferred_element_type=jnp.float32
        )
        back = jnp.concatenate(
            [
                rotate(grad_queries, cosine, -sine_table).reshape(length, span),
                rotate(grad_keys, cosine, -sine_table).reshape(length, span),
                grad_values.reshape(length, span),
            ],
            axis=1,
        ).astype(low)
        grad_normed_attn = scatter_sum(against(back, attn_weight), members)
        grad_attn_weight = swap(
            over_rows(normed_attn, back).astype(low).reshape(members, own_rows, 3 * span)
        )
        gain_sums[layer] = jnp.sum(grad_normed_attn * unit_attn, axis=0)
        grad_result = grad_after + norm_back(
            grad_normed_attn * gains[layer], unit_attn, inverse_attn
        )

        before = lax.ppermute(
            grad_out, "group", [(member, member + 1) for member in range(members - 1)]
        )
        own_out = lax.dynamic_slice_in_dim(
            jnp.concatenate([before, grad_out], axis=0),
            span - owner * (span - own_rows),
            own_rows,
            0,
        )

        def narrow(blocks):
            wide = by_row(blocks)[:, : HEADS * HEAD_DIM].astype(jnp.float32)
            wide = wide.reshape(own_rows, KV_HEADS, SHARE, HEAD_DIM)
            return wide.sum(axis=2).reshape(own_rows, KV_HEADS * HEAD_DIM).astype(low)

        shares = (
            by_row(grad_attn_weight[:, :, :span])[:, : HEADS * HEAD_DIM],
            narrow(grad_attn_weight[:, :, span : 2 * span]),
            narrow(grad_attn_weight[:, :, 2 * span :]),
            own_out,
            by_row(grad_ffn_weight[:, :, :part_ff]),
            by_row(grad_ffn_weight[:, :, part_ff:]),
            grad_down,
        )
        if layer + 1 < LAYERS:
            shares, owned[layer + 1] = lax.optimization_barrier((shares, owned[layer + 1]))
        owned[layer] = lax.psum(shares, "replica")

    gain_total = lax.psum(jnp.stack(gain_sums), ("group", "replica"))
    gain_total = lax.dynamic_slice_in_dim(gain_total, owner * own_rows, own_rows, 1)
    stacked = [
        jnp.stack([owned[layer][place] for layer in range(LAYERS)]).astype(jnp.float32)
        for place in range(7)
    ]
    return (
        jnp.stack(outputs)[None],
        grad_result[None],
        gain_total[:LAYERS],
        stacked[0],
        stacked[1],
        stacked[2],
        stacked[3],
        gain_total[LAYERS:],
        stacked[4],
        stacked[5],
        stacked[6],
    )


def solution(mesh):
    rows = P(None, "group", None)
    in_specs = (
        P("replica", "group", None),
        P("replica", "group"),
        P(None, "group"),
        rows,
        rows,
        rows,
        rows,
        P(None, "group"),
        rows,
        rows,
        rows,
        P("replica", "group", None),
    )
    out_specs = (
        P("replica", None, "group", None),
        P("replica", "group", None),
        P(None, "group"),
        rows,
        rows,
        rows,
        rows,
        P(None, "group"),
        rows,
        rows,
        rows,
    )
    return jax.shard_map(
        on_device, mesh=mesh, in_specs=in_specs, out_specs=out_specs, check_vma=False
    )
```

time: 1600 us -> 743 us (0.46)
  waiting for transfers between devices: 1100 us -> 125 us
  Pallas kernels: 0 us -> 267 us
  blocking collectives: 205 us -> 66.5 us
  matrix products: 191 us -> 91.5 us
  local copies, waits for them, and re-layouts: 36.4 us -> 82.4 us
  starting transfers between devices: 1.46 us -> 46.9 us
    all_gather x28 -> x0, waiting for transfers between devices: 638 us -> none  [the longest x2 86.6 us: layer_backward(): piece_up = lax.all_gather(grad_up_low, 'group', axis=0, tiled=True)]
    pallas_call x0 -> x16, Pallas kernels: none -> 267 us  [the longest x8 136 us: scatter_sum(): pl.pallas_call(lambda *refs: scatter_kernel(members, *refs), out_shape=ja...]
    psum x1 -> x2, waiting for transfers between devices: 311 us -> 104 us  [on_device(): owned[layer] = lax.psum(shares, 'replica')]
    reduce_scatter x4 -> x0, waiting for transfers between devices: 141 us -> none  [the longest x2 75.5 us: layer_backward(): lax.psum_scatter(grad_value_all, 'group', scatter_dimension=0, tiled=True)]
    all_gather x12 -> x2, blocking collectives: 154 us -> 25.2 us  [the longest x1 15.8 us: on_device(): all_positions = lax.all_gather(positions[0], 'group', axis=0, tiled=True)]
    dot_general x24 -> x18, matrix products: 86.3 us -> 35.1 us  [the longest x8 19.8 us: dot(): return jnp.dot(left, right, preferred_element_type=jnp.float32)]
    all_to_all x0 -> x8, starting transfers between devices: none -> 40.6 us  [swap(): lax.all_to_all(blocks, 'group', split_axis=0, concat_axis=0, tiled=True)]
    unnamed x2 -> x0, blocking collectives: 40.2 us -> none
  transfers between devices with their start and end apart: 33 -> 13, of which waited for: 27 -> 6; matrix products, arithmetic and copies ran while one was open for 13% -> 17% of each run, Pallas kernels for 0% -> 21%
where the time goes in v1:
time: 743 us; the launch traced here: 735 us
  Pallas kernels  267 us (36%)
  waiting for transfers between devices  125 us (17%)
  matrix products  91.5 us (12%)
  local copies, waits for them, and re-layouts  82.4 us (11%)
  blocking collectives  66.5 us (9%)
  starting transfers between devices  46.9 us (6%)
  other arithmetic  38.7 us (5%)
  between operations  16.3 us (2%)
    pallas_call x8, Pallas kernels, scatter_sum(): pl.pallas_call(lambda *refs: scatter_kernel(members, *refs), out_shape=ja...  136 us
    pallas_call x8, Pallas kernels, gather(): pl.pallas_call(lambda *refs: gather_kernel(members, *refs), out_shape=jax...  131 us
    psum x2, waiting for transfers between devices, on_device(): owned[layer] = lax.psum(shares, 'replica')  104 us
    psum x1, blocking collectives, on_device(): gain_total = lax.psum(jnp.stack(gain_sums), ('group', 'replica'))  41.3 us
    all_to_all x8, starting transfers between devices, swap(): lax.all_to_all(blocks, 'group', split_axis=0, concat_axis=0, tiled=True)  40.6 us
    unnamed x260, local copies, waits for them, and re-layouts  30.3 us
    dot_general x8, matrix products, over_rows(): lax.dot_general(left, right, (((0,), (0,)), ((), ())), preferred_element_...  23.4 us
    convert_element_type x8, local copies, waits for them, and re-layouts, scatter_sum(): partial.astype(low).reshape(members, rows, width)  22.7 us
  transfers between devices with their start and end apart: 13, of which 6 were waited for; matrix products, arithmetic and copies ran while one was open for 17% of the time, Pallas kernels for 21%

profile of v1, /device:TPU:0, one launch (start us, length us, event | category | flops | bytes accessed | tf_op | source)
XLA Modules:
  0.0 734.7 jit_solution(7637742487808334804)
XLA Ops:
  17.2 15.8 %all-gather = s32[1,1024]{1,0:T(1,128)S(1)} all-gather(s32[1,128]{1,0:T(1,128)S(1)} %copy-done.107), channel_id=2, replica_groups=mesh['group'=8,'replica'=4] {'group'}, dimensions={1}, use_global_device_ids=true | all-gather | bytes 4608 | tf_op jit(solution)/shard_map/all_gather | solution.py:258
  35.0 9.4 %all-gather.1 = bf16[8,120,4]{1,2,0:T(4,128)(2,1)S(1)} all-gather(bf16[1,120,4]{1,2,0:T(4,128)(2,1)S(1)} %maximum_bitcast_fusion.1), channel_id=1, replica_groups=mesh['group'=8,'replica'=4] {'group'}, dimensions={0}, use_global_device_ids=true | all-gather | bytes 8640 | tf_op jit(solution)/shard_map/all_gather | solution.py:259
  57.4 16.8 %shard_map.203 = bf16[8,128,960]{2,1,0:T(8,128)(2,1)S(1)} custom-call(bf16[128,960]{1,0:T(8,128)(2,1)S(1)} %fusion.33.refs_0_), custom_call_target="tpu_custom_call" | custom-call | bytes 30000000 | tf_op jit(solution)/shard_map/pallas_call | solution.py:90
  80.9 16.5 %shard_map.211 = bf16[8,128,960]{2,1,0:T(8,128)(2,1)S(1)} custom-call(bf16[128,960]{1,0:T(8,128)(2,1)S(1)} %bitcast.307), custom_call_target="tpu_custom_call" | custom-call | bytes 30000000 | tf_op jit(solution)/shard_map/pallas_call | solution.py:90
  109.7 6.8 fusion.83
  128.8 17.4 %shard_map.204 = f32[128,960]{1,0:T(8,128)S(1)} custom-call(bf16[8,128,960]{2,1,0:T(8,128)(2,1)S(1)} %bitcast.299), custom_call_target="tpu_custom_call" | custom-call | bytes 30000000 | tf_op jit(solution)/shard_map/pallas_call | solution.py:161
  147.2 16.5 %shard_map.205 = bf16[8,128,960]{2,1,0:T(8,128)(2,1)S(1)} custom-call(bf16[128,960]{1,0:T(8,128)(2,1)S(1)} %multiply_convert_fusion.10.refs_0_), custom_call_target="tpu_custom_call" | custom-call | bytes 30000000 | tf_op jit(solution)/shard_map/pallas_call | solution.py:90
  178.6 17.4 %shard_map.206 = f32[128,960]{1,0:T(8,128)S(1)} custom-call(bf16[8,128,960]{2,1,0:T(8,128)(2,1)S(1)} %bitcast.300), custom_call_target="tpu_custom_call" | custom-call | bytes 30000000 | tf_op jit(solution)/shard_map/pallas_call | solution.py:161
  196.3 16.5 %shard_map.207 = bf16[8,128,960]{2,1,0:T(8,128)(2,1)S(1)} custom-call(bf16[128,960]{1,0:T(8,128)(2,1)S(1)} %multiply_convert_fusion.9.refs_0_), custom_call_target="tpu_custom_call" | custom-call | bytes 30000000 | tf_op jit(solution)/shard_map/pallas_call | solution.py:90
  238.3 17.4 %shard_map.208 = f32[128,960]{1,0:T(8,128)S(1)} custom-call(bf16[8,128,960]{2,1,0:T(8,128)(2,1)S(1)} %bitcast.301), custom_call_target="tpu_custom_call" | custom-call | bytes 30000000 | tf_op jit(solution)/shard_map/pallas_call | solution.py:161
  256.6 16.5 %shard_map.209 = bf16[8,128,960]{2,1,0:T(8,128)(2,1)S(1)} custom-call(bf16[128,960]{1,0:T(8,128)(2,1)S(1)} %multiply_convert_fusion.8.refs_0_), custom_call_target="tpu_custom_call" | custom-call | bytes 30000000 | tf_op jit(solution)/shard_map/pallas_call | solution.py:90
  287.3 16.9 %shard_map.212 = f32[128,960]{1,0:T(8,128)S(1)} custom-call(bf16[8,128,960]{2,1,0:T(8,128)(2,1)S(1)} %bitcast.302), custom_call_target="tpu_custom_call" | custom-call | bytes 30000000 | tf_op jit(solution)/shard_map/pallas_call | solution.py:161
  305.7 16.1 %shard_map.213 = bf16[8,128,960]{2,1,0:T(8,128)(2,1)S(1)} custom-call(bf16[128,960]{1,0:T(8,128)(2,1)S(1)} %fusion.72.refs_0_), custom_call_target="tpu_custom_call" | custom-call | bytes 30000000 | tf_op jit(solution)/shard_map/pallas_call | solution.py:90
  339.4 16.7 %shard_map.214 = f32[128,960]{1,0:T(8,128)S(1)} custom-call(bf16[8,128,960]{2,1,0:T(8,128)(2,1)S(1)} %bitcast.303), custom_call_target="tpu_custom_call" | custom-call | bytes 30000000 | tf_op jit(solution)/shard_map/pallas_call | solution.py:161
  362.8 16.7 %shard_map.210 = f32[128,960]{1,0:T(8,128)S(1)} custom-call(bf16[8,128,960]{2,1,0:T(8,128)(2,1)S(1)} %bitcast.304), custom_call_target="tpu_custom_call" | custom-call | bytes 30000000 | tf_op jit(solution)/shard_map/pallas_call | solution.py:161
  380.8 15.9 %shard_map.215 = bf16[8,128,960]{2,1,0:T(8,128)(2,1)S(1)} custom-call(bf16[128,960]{1,0:T(8,128)(2,1)S(1)} %get-tuple-element.129.refs_0_), custom_call_target="tpu_custom_call" | custom-call | bytes 30000000 | tf_op jit(solution)/shard_map/pallas_call | solution.py:90
  406.2 16.8 %shard_map.216 = f32[128,960]{1,0:T(8,128)S(1)} custom-call(bf16[8,128,960]{2,1,0:T(8,128)(2,1)S(1)} %bitcast.305), custom_call_target="tpu_custom_call" | custom-call | bytes 30000000 | tf_op jit(solution)/shard_map/pallas_call | solution.py:161
  424.3 16.1 %shard_map.217 = bf16[8,128,960]{2,1,0:T(8,128)(2,1)S(1)} custom-call(bf16[128,960]{1,0:T(8,128)(2,1)S(1)} %get-tuple-element.127.refs_0_), custom_call_target="tpu_custom_call" | custom-call | bytes 30000000 | tf_op jit(solution)/shard_map/pallas_call | solution.py:90
  495.7 9.2 %all-to-all-start.4 = ((bf16[8,120,384]{2,1,0:T(8,128)(2,1)}), bf16[8,120,384]{2,1,0:T(8,128)(2,1)}, u32[]{:S(2)}, u32[]{:S(2)}) async-start(bf16[8,120,384]{2,1,0:T(8,128)(2,1)} %bitcast.373), calls=%async_computation.4 | async-start | bytes 1474560 | tf_op jit(solution)/shard_map/all_to_all | solution.py:182
  509.7 7.4 %all-to-all-done.4 = bf16[8,120,384]{2,1,0:T(8,128)(2,1)} async-done(((bf16[8,120,384]{2,1,0:T(8,128)(2,1)}), bf16[8,120,384]{2,1,0:T(8,128)(2,1)}, u32[]{:S(2)}, u32[]{:S(2)}) %all-to-all-start.4) | async-done | bytes 737312 | tf_op jit(solution)/shard_map/all_to_all | solution.py:182
  542.7 62.0 %all-reduce.13.cloned.1.call-done = (bf16[120,960]{1,0:T(8,128)(2,1)}, bf16[120,320]{0,1:T(8,128)(2,1)}, bf16[120,320]{0,1:T(8,128)(2,1)}, bf16[120,960]{0,1:T(8...) async-done(((bf16[120,960]{1,0:T(8,128)(2,1)}, bf16[120,320]{0,1:T(8,128)(2,1)}, bf16[120,320]{0,1:T(8,128)(2,1)}, ...) | async-done | bytes 2457616 | tf_op jit(solution)/shard_map/psum | solution.py:417
  611.1 16.9 %shard_map.218 = f32[128,960]{1,0:T(8,128)S(1)} custom-call(bf16[8,128,960]{2,1,0:T(8,128)(2,1)S(1)} %bitcast.306), custom_call_target="tpu_custom_call" | custom-call | bytes 30000000 | tf_op jit(solution)/shard_map/pallas_call | solution.py:161
  631.0 41.3 %psum.105 = f32[4,960]{1,0:T(4,128)S(1)} all-reduce(f32[4,960]{1,0:T(4,128)S(1)} %pad_maximum_fusion.48), channel_id=1, replica_groups=mesh['group'=8,'replica'=4] {'group','replica'}, use_global_device_ids=true, to_apply=%region_18.19 | all-reduce | flops 3840 | bytes 30720 | tf_op jit(solution)/shard_map/psum | solution.py:419
  673.0 41.9 %all-reduce.11.cloned.1.call-done = (bf16[1,120,960]{2,1,0:T(8,128)(2,1)}, bf16[1,120,320]{1,2,0:T(8,128)(2,1)}, bf16[1,120,320]{1,2,0:T(8,128)(2,1)}, bf16[1,12...) async-done(((bf16[1,120,960]{2,1,0:T(8,128)(2,1)}, bf16[1,120,320]{1,2,0:T(8,128)(2,1)}, ...) | async-done | bytes 2457616 | tf_op jit(solution)/shard_map/psum | solution.py:417
  (436 shorter events, 257.4 us)
Async XLA Ops:
  9.1 25.1 %copy-start.78 = (bf16[1,128,960]{1,2,0:T(8,128)(2,1)S(1)}, bf16[1,128,960]{1,2,0:T(8,128)(2,1)}, u32[]{:S(2)}) copy-start(bf16[1,128,960]{1,2,0:T(8,128)(2,1)} %param.12) | copy-start | bytes 737284
  9.2 25.8 %copy-start.108 = (bf16[2,120]{1,0:T(2,128)(2,1)S(1)}, bf16[2,120]{1,0:T(2,128)(2,1)}, u32[]{:S(2)}) copy-start(bf16[2,120]{1,0:T(2,128)(2,1)} %param.19) | copy-start | bytes 1444
  9.3 25.8 %copy-start.109 = (bf16[2,120]{1,0:T(2,128)(2,1)S(1)}, bf16[2,120]{1,0:T(2,128)(2,1)}, u32[]{:S(2)}) copy-start(bf16[2,120]{1,0:T(2,128)(2,1)} %param.14) | copy-start | bytes 1444
  10.2 91.4 %all-to-all-start = ((bf16[8,120,384]{2,1,0:T(8,128)(2,1)}), bf16[8,120,384]{2,1,0:T(8,128)(2,1)}, u32[]{:S(2)}, u32[]{:S(2)}) async-start(bf16[8,120,384]{2,1,0:T(8,128)(2,1)} %copy.252), calls=%async_computation | async-start | bytes 1474560 | tf_op jit(solution)/shard_map/all_to_all | solution.py:182
  15.4 84.9 %collective-permute-start = (bf16[2,120,960]{2,1,0:T(8,128)(2,1)}, bf16[2,120,960]{2,1,0:T(8,128)(2,1)}, u32[]{:S(2)}, u32[]{:S(2)}) collective-permute-start(bf16[2,120,960]{2,1,0:T(8,128)(2,1)} %param.18), channel_id=1, source_target_pairs={{4,0},{8,4},{12,8},{16,12},{20,16},{24,20},{28,24},{5,1},{9,5},{13... | collective-permute-start | bytes 1382408 | tf_op jit(solution)/shard_map/ppermute | solution.py:279
  34.3 111.9 %copy-start.23 = (bf16[1,128,960]{2,1,0:T(8,128)(2,1)}, bf16[1,128,960]{2,1,0:T(8,128)(2,1)S(1)}, u32[]{:S(2)}) copy-start(bf16[1,128,960]{2,1,0:T(8,128)(2,1)S(1)} %copy.248) | copy-start | bytes 737284
  74.2 32.3 %copy-start.1 = (bf16[8,128,960]{2,1,0:T(8,128)(2,1)}, bf16[8,128,960]{2,1,0:T(8,128)(2,1)S(1)}, u32[]{:S(2)}) copy-start(bf16[8,128,960]{2,1,0:T(8,128)(2,1)S(1)} %shard_map.203) | copy-start | bytes 5898244
  78.3 20.5 %copy-start.90 = (s32[1024]{0:T(1024)S(1)}, s32[1024]{0:T(1024)}, u32[]{:S(2)}) copy-start(s32[1024]{0:T(1024)} %iota_subtract_fusion) | copy-start | bytes 12292
  101.6 21.6 %copy-start.37 = (bf16[2,128,960]{2,1,0:T(8,128)(2,1)}, bf16[2,128,960]{2,1,0:T(8,128)(2,1)S(1)}, u32[]{:S(2)}) copy-start(bf16[2,128,960]{2,1,0:T(8,128)(2,1)S(1)} %fusion.42) | copy-start | bytes 1474564
  101.7 62.0 %all-to-all-start.1 = ((bf16[8,120,640]{2,1,0:T(8,128)(2,1)}), bf16[8,120,640]{2,1,0:T(8,128)(2,1)}, u32[]{:S(2)}, u32[]{:S(2)}) async-start(bf16[8,120,640]{2,1,0:T(8,128)(2,1)} %copy.257), calls=%async_computation.1 | async-start | bytes 2457600 | tf_op jit(solution)/shard_map/all_to_all | solution.py:182
  146.4 49.5 %copy-start.19 = (f32[128,960]{1,0:T(8,128)}, f32[128,960]{1,0:T(8,128)S(1)}, u32[]{:S(2)}) copy-start(f32[128,960]{1,0:T(8,128)S(1)} %get-tuple-element.136) | copy-start | bytes 1474564
  163.7 49.1 %all-to-all-start.2 = ((bf16[8,120,384]{2,1,0:T(8,128)(2,1)}), bf16[8,120,384]{2,1,0:T(8,128)(2,1)}, u32[]{:S(2)}, u32[]{:S(2)}) async-start(bf16[8,120,384]{2,1,0:T(8,128)(2,1)} %copy.261), calls=%async_computation.2 | async-start | bytes 1474560 | tf_op jit(solution)/shard_map/all_to_all | solution.py:182
  196.1 59.6 %copy-start.15 = (f32[128,960]{1,0:T(8,128)}, f32[128,960]{1,0:T(8,128)S(1)}, u32[]{:S(2)}) copy-start(f32[128,960]{1,0:T(8,128)S(1)} %get-tuple-element.134) | copy-start | bytes 1474564
  212.8 60.3 %all-to-all-start.3 = ((bf16[8,120,640]{2,1,0:T(8,128)(2,1)}), bf16[8,120,640]{2,1,0:T(8,128)(2,1)}, u32[]{:S(2)}, u32[]{:S(2)}) async-start(bf16[8,120,640]{2,1,0:T(8,128)(2,1)} %copy.266), calls=%async_computation.3 | async-start | bytes 2457600 | tf_op jit(solution)/shard_map/all_to_all | solution.py:182
  255.9 49.1 %copy-start.21 = (f32[128,960]{1,0:T(8,128)}, f32[128,960]{1,0:T(8,128)S(1)}, u32[]{:S(2)}) copy-start(f32[128,960]{1,0:T(8,128)S(1)} %get-tuple-element.132) | copy-start | bytes 1474564
  445.8 16.3 %all-to-all-start.6 = ((bf16[8,120,384]{2,1,0:T(8,128)(2,1)}), bf16[8,120,384]{2,1,0:T(8,128)(2,1)}, u32[]{:S(2)}, u32[]{:S(2)}) async-start(bf16[8,120,384]{2,1,0:T(8,128)(2,1)} %bitcast.372), calls=%async_computation.6 | async-start | bytes 1474560 | tf_op jit(solution)/shard_map/all_to_all | solution.py:182
  462.1 21.6 %all-to-all-start.7 = ((bf16[8,120,640]{2,1,0:T(8,128)(2,1)}), bf16[8,120,640]{2,1,0:T(8,128)(2,1)}, u32[]{:S(2)}, u32[]{:S(2)}) async-start(bf16[8,120,640]{2,1,0:T(8,128)(2,1)} %bitcast.341), calls=%async_computation.7 | async-start | bytes 2457600 | tf_op jit(solution)/shard_map/all_to_all | solution.py:182
  466.3 138.3 %all-reduce.13.cloned.1.call-start = ((), (), s32[]{:S(2)}) async-start(), calls=%async_computation.9 | async-start | bytes 5242880 | tf_op jit(solution)/shard_map/psum | solution.py:417
  469.0 7.8 %collective-permute-start.2 = (bf16[128,960]{0,1:T(8,128)(2,1)S(1)}, bf16[128,960]{0,1:T(8,128)(2,1)S(1)}, u32[]{:S(2)}, u32[]{:S(2)}) collective-permute-start(bf16[128,960]{0,1:T(8,128)(2,1)S(1)} %convolution_convert_fusion.20), channel_id=1, source_target_pairs={{0,4},{4,8},{8,12},{12,16},{16,20},{20,24},{24,28},{1,5},{5,9},{9,... | collective-permute-start | bytes 737288 | tf_op jit(solution)/shard_map/ppermute | solution.py:391
  495.7 21.4 %all-to-all-start.4 = ((bf16[8,120,384]{2,1,0:T(8,128)(2,1)}), bf16[8,120,384]{2,1,0:T(8,128)(2,1)}, u32[]{:S(2)}, u32[]{:S(2)}) async-start(bf16[8,120,384]{2,1,0:T(8,128)(2,1)} %bitcast.373), calls=%async_computation.4 | async-start | bytes 1474560 | tf_op jit(solution)/shard_map/all_to_all | solution.py:182
  517.1 21.6 %all-to-all-start.5 = ((bf16[8,120,640]{2,1,0:T(8,128)(2,1)}), bf16[8,120,640]{2,1,0:T(8,128)(2,1)}, u32[]{:S(2)}, u32[]{:S(2)}) async-start(bf16[8,120,640]{2,1,0:T(8,128)(2,1)} %bitcast.342), calls=%async_computation.5 | async-start | bytes 2457600 | tf_op jit(solution)/shard_map/all_to_all | solution.py:182
  521.4 193.5 %all-reduce.11.cloned.1.call-start = ((), (), s32[]{:S(2)}) async-start(), calls=%async_computation.8 | async-start | bytes 5242880 | tf_op jit(solution)/shard_map/psum | solution.py:417
  522.4 5.3 collective-permute-start.1
  629.6 85.2 %copy-start.55 = (bf16[120,2560]{0,1:T(8,128)(2,1)S(1)}, bf16[120,2560]{0,1:T(8,128)(2,1)}, u32[]{:S(2)}) copy-start(bf16[120,2560]{0,1:T(8,128)(2,1)} %get-tuple-element.36) | copy-start | bytes 1843204
  (111 other events, 696.2 us)
Sparse Core Ops, SparseCore 0:
  491.2 113.4 all-reduce.12
  608.8 106.0 all-reduce.10

commit v2 on v1

--- a/solution.py
+++ b/solution.py
@@ -32,17 +32,18 @@
     )
 
 
-def gather_kernel(members, block_ref, out_ref, local_sem, send_sem, recv_sem, pass_sem, got_sem):
-    me = lax.axis_index("group")
-    chips = members // 2
-    chip, core = lax.div(me, 2), lax.rem(me, 2)
-    sibling = chip * 2 + 1 - core
+def greet(chips, chip, core, sibling):
     barrier = pltpu.get_barrier_semaphore()
     pl.semaphore_signal(barrier, inc=1, device_id={"group": sibling})
     for step in range(1, chips):
         peer = lax.rem(chip + step, chips) * 2 + core
         pl.semaphore_signal(barrier, inc=1, device_id={"group": peer})
-    pl.semaphore_wait(barrier, chips)
+    return barrier
+
+
+def spread(chips, me, block_ref, out_ref, local_sem, send_sem, recv_sem, pass_sem, got_sem):
+    chip, core = lax.div(me, 2), lax.rem(me, 2)
+    sibling = chip * 2 + 1 - core
     sends = []
     for step in range(1, chips):
         peer = lax.rem(chip + step, chips) * 2 + core
@@ -85,43 +86,97 @@
         copy.wait_send()
 
 
-def gather(block, members):
-    rows, width = block.shape
-    out = pl.pallas_call(
-        lambda *refs: gather_kernel(members, *refs),
-        out_shape=jax.ShapeDtypeStruct((members, rows, width), block.dtype),
-        in_specs=[pl.BlockSpec(memory_space=pltpu.VMEM)],
-        out_specs=pl.BlockSpec(memory_space=pltpu.VMEM),
-        scratch_shapes=[pltpu.SemaphoreType.DMA]
-        + [pltpu.SemaphoreType.DMA((members // 2,)) for _ in range(4)],
+def first_kernel(
+    members, block_ref, small_ref, weight_ref, out_ref, few_ref, swapped_ref,
+    local_sem, send_sem, recv_sem, pass_sem, got_sem, few_sem, few_recv, swap_sem, swap_recv, own_sem,
+):
+    me = lax.axis_index("group")
+    chips = members // 2
+    barrier = pltpu.get_barrier_semaphore()
+    for step in range(1, members):
+        peer = lax.rem(me + step, members)
+        pl.semaphore_signal(barrier, inc=1, device_id={"group": peer})
+    pl.semaphore_wait(barrier, members - 1)
+    copies = []
+    for step in range(1, members):
+        peer = lax.rem(me + step, members)
+        few = pltpu.make_async_remote_copy(
+            src_ref=small_ref,
+            dst_ref=few_ref.at[me],
+            send_sem=few_sem.at[step],
+            recv_sem=few_recv.at[step],
+            device_id={"group": peer},
+        )
+        few.start()
+        block = pltpu.make_async_remote_copy(
+            src_ref=weight_ref.at[peer],
+            dst_ref=swapped_ref.at[me],
+            send_sem=swap_sem.at[step],
+            recv_sem=swap_recv.at[step],
+            device_id={"group": peer},
+        )
+        block.start()
+        copies += [few, block]
+    own_few = pltpu.make_async_copy(small_ref, few_ref.at[me], own_sem.at[0])
+    own_few.start()
+    own_block = pltpu.make_async_copy(weight_ref.at[me], swapped_ref.at[me], own_sem.at[1])
+    own_block.start()
+    spread(chips, me, block_ref, out_ref, local_sem, send_sem, recv_sem, pass_sem, got_sem)
+    own_few.wait()
+    own_block.wait()
+    for copy in copies:
+        copy.wait()
+
+
+def vmem():
+    return pl.BlockSpec(memory_space=pltpu.VMEM)
+
+
+def first_exchange(block, small, weight, members):
+    sems = pltpu.SemaphoreType.DMA((members,))
+    return pl.pallas_call(
+        lambda *refs: first_kernel(members, *refs),
+        out_shape=[
+            jax.ShapeDtypeStruct((members,) + block.shape, block.dtype),
+            jax.ShapeDtypeStruct((members,) + small.shape, small.dtype),
+            jax.ShapeDtypeStruct(weight.shape, weight.dtype),
+        ],
+        in_specs=[vmem()] * 3,
+        out_specs=[vmem()] * 3,
+        scratch_shapes=[pltpu.SemaphoreType.DMA] + [sems] * 8 + [pltpu.SemaphoreType.DMA((2,))],
         compiler_params=pltpu.CompilerParams(
             collective_id=0, has_side_effects=True, vmem_limit_bytes=24 * 2**20
         ),
-        cost_estimate=pl.CostEstimate(
-            flops=0, bytes_accessed=30_000_000, transcendentals=0
-        ),
-    )(block)
-    return out.reshape(members * rows, width)
-
-
-def scatter_kernel(
-    members, part_ref, out_ref, pair_ref, ready_ref, land_ref, pair_send, pair_recv, send_sem, recv_sem
-):
+        cost_estimate=pl.CostEstimate(flops=0, bytes_accessed=60_000_000, transcendentals=0),
+    )(block, small, weight)
+
+
+def sum_kernel(members, backward, gathers, *refs):
+    refs = list(refs)
+    left_ref, right_ref, stream_ref, gain_ref = refs[:4]
+    refs = refs[4:]
+    if backward:
+        grad_ref = refs.pop(0)
+    result_ref = refs.pop(0)
+    if backward:
+        gain_out_ref = refs.pop(0)
+    if gathers:
+        out_ref = refs.pop(0)
+    give_ref, pair_ref, ready_ref, land_ref, total_ref, low_ref = refs[:6]
+    pair_send, pair_recv, send_sem, recv_sem = refs[6:10]
     me = lax.axis_index("group")
     chips = members // 2
     chip, core = lax.div(me, 2), lax.rem(me, 2)
     sibling = chip * 2 + 1 - core
-    barrier = pltpu.get_barrier_semaphore()
-    pl.semaphore_signal(barrier, inc=1, device_id={"group": sibling})
-    for step in range(1, chips):
-        peer = lax.rem(chip + step, chips) * 2 + core
-        pl.semaphore_signal(barrier, inc=1, device_id={"group": peer})
-    pl.semaphore_wait(barrier, chips)
+    barrier = greet(chips, chip, core, sibling)
     pairs = []
     for step in range(chips):
         place = lax.rem(chip + step + 1, chips)
+        give_ref[step] = dot(left_ref[place * 2 + 1 - core], right_ref[...]).astype(low)
+        if step == 0:
+            pl.semaphore_wait(barrier, chips)
         copy = pltpu.make_async_remote_copy(
-            src_ref=part_ref.at[place * 2 + 1 - core],
+            src_ref=give_ref.at[step],
             dst_ref=pair_ref.at[step],
             send_sem=pair_send.at[step],
             recv_sem=pair_recv.at[step],
@@ -132,12 +187,13 @@
     sends = []
     for step in range(chips):
         place = lax.rem(chip + step + 1, chips)
+        part = dot(left_ref[place * 2 + core], right_ref[...])
         pairs[step].wait_recv()
-        total = part_ref[place * 2 + core].astype(jnp.float32) + pair_ref[step].astype(jnp.float32)
+        part = part + pair_ref[step].astype(jnp.float32)
         if step == chips - 1:
-            out_ref[...] = total
+            total_ref[...] = part
             break
-        ready_ref[step] = total.astype(low)
+        ready_ref[step] = part.astype(low)
         copy = pltpu.make_async_remote_copy(
             src_ref=ready_ref.at[step],
             dst_ref=land_ref.at[step],
@@ -149,33 +205,59 @@
         sends.append(copy)
     for step in range(chips - 1):
         sends[step].wait_recv()
-        out_ref[...] += land_ref[step].astype(jnp.float32)
+        total_ref[...] += land_ref[step].astype(jnp.float32)
+    total = total_ref[...]
+    if backward:
+        inverse, unit = norm_forward(stream_ref[...])
+        gain_out_ref[...] = jnp.sum(total * unit, axis=0, keepdims=True)
+        result = grad_ref[...] + norm_back(total * gain_ref[...], unit, inverse)
+        result_ref[...] = result
+        low_ref[...] = result.astype(low)
+    else:
+        result = stream_ref[...] + total
+        result_ref[...] = result
+        if gathers:
+            unit = norm_forward(result)[1]
+            low_ref[...] = (unit * gain_ref[...]).astype(low)
+    if gathers:
+        spread(chips, me, low_ref, out_ref, *refs[10:])
     for copy in pairs + sends:
         copy.wait_send()
 
 
-def scatter_sum(partial, members):
-    length, width = partial.shape
-    rows = length // members
+def block_sum(name, left, right, stream, gain, members, grad=None, gathers=True):
+    rows, width = stream.shape
     chips = members // 2
-    return pl.pallas_call(
-        lambda *refs: scatter_kernel(members, *refs),
-        out_shape=jax.ShapeDtypeStruct((rows, width), jnp.float32),
-        in_specs=[pl.BlockSpec(memory_space=pltpu.VMEM)],
-        out_specs=pl.BlockSpec(memory_space=pltpu.VMEM),
-        scratch_shapes=[
-            pltpu.VMEM((chips, rows, width), low),
-            pltpu.VMEM((chips, rows, width), low),
-            pltpu.VMEM((chips, rows, width), low),
-        ]
-        + [pltpu.SemaphoreType.DMA((chips,)) for _ in range(4)],
+    backward = grad is not None
+    outs = [jax.ShapeDtypeStruct((rows, width), jnp.float32)]
+    if backward:
+        outs.append(jax.ShapeDtypeStruct((1, width), jnp.float32))
+    if gathers:
+        outs.append(jax.ShapeDtypeStruct((members, rows, width), low))
+    operands = [left.reshape(members, rows, left.shape[1]), right, stream, gain[None]]
+    if backward:
+        operands.append(grad)
+    sems = pltpu.SemaphoreType.DMA((chips,))
+    scratch = [pltpu.VMEM((chips, rows, width), low) for _ in range(4)]
+    scratch += [pltpu.VMEM((rows, width), jnp.float32), pltpu.VMEM((rows, width), low)]
+    scratch += [sems] * 4
+    if gathers:
+        scratch += [pltpu.SemaphoreType.DMA] + [sems] * 4
+    result = pl.pallas_call(
+        lambda *refs: sum_kernel(members, backward, gathers, *refs),
+        out_shape=outs,
+        in_specs=[vmem()] * len(operands),
+        out_specs=[vmem()] * len(outs),
+        scratch_shapes=scratch,
         compiler_params=pltpu.CompilerParams(
-            collective_id=1, has_side_effects=True, vmem_limit_bytes=24 * 2**20
+            collective_id=name, has_side_effects=True, vmem_limit_bytes=32 * 2**20
         ),
-        cost_estimate=pl.CostEstimate(
-            flops=0, bytes_accessed=30_000_000, transcendentals=0
-        ),
-    )(partial.astype(low).reshape(members, rows, width))
+        cost_estimate=pl.CostEstimate(flops=0, bytes_accessed=90_000_000, transcendentals=0),
+    )(*operands)
+    result = list(result)
+    if gathers:
+        result[-1] = result[-1].reshape(members * rows, width)
+    return result
 
 
 def swap(blocks):
@@ -255,14 +337,8 @@
     padded = span * members
     part_ff = w_gate.shape[2] // members
 
-    all_positions = lax.all_gather(positions[0], "group", axis=0, tiled=True)
-    gains = lax.all_gather(
-        jnp.concatenate([gain_attn, gain_ffn], axis=0), "group", axis=1, tiled=True
-    ).astype(jnp.float32)
-
-    weights = []
-    for layer in range(LAYERS):
-        attn_blocks = jnp.concatenate(
+    def attn_blocks(layer):
+        return jnp.concatenate(
             [
                 by_member(pad_columns(w_query[layer], padded), members),
                 by_member(pad_columns(widen(w_key[layer]), padded), members),
@@ -270,12 +346,32 @@
             ],
             axis=2,
         )
-        ffn_blocks = jnp.concatenate(
+
+    def ffn_blocks(layer):
+        return jnp.concatenate(
             [by_member(w_gate[layer], members), by_member(w_up[layer], members)], axis=2
         )
-        attn_weight = swap(attn_blocks).reshape(width, 3 * span)
-        ffn_weight = swap(ffn_blocks).reshape(width, 2 * part_ff)
-        weights.append([attn_weight, ffn_weight])
+
+    lane = 128 * -(-max(row_count, own_rows) // 128)
+    small = jnp.concatenate(
+        [
+            pad_columns(positions.astype(jnp.float32), lane),
+            pad_columns(gain_attn.astype(jnp.float32), lane),
+            pad_columns(gain_ffn.astype(jnp.float32), lane),
+        ],
+        axis=0,
+    )
+    small = jnp.pad(small, ((0, 8 - small.shape[0]), (0, 0)))
+    token_blocks, few, first_weight = first_exchange(tokens[0], small, attn_blocks(0), members)
+    all_positions = few[:, 0, :row_count].reshape(length).astype(jnp.int32)
+    gains = few[:, 1 : 1 + 2 * LAYERS, :own_rows].transpose(1, 0, 2).reshape(2 * LAYERS, width)
+    out_low = lax.all_gather(cotangent[0], "group", axis=0, tiled=True)
+
+    weights = []
+    for layer in range(LAYERS):
+        attn_weight = first_weight if layer == 0 else swap(attn_blocks(layer))
+        ffn_weight = swap(ffn_blocks(layer)).reshape(width, 2 * part_ff)
+        weights.append([attn_weight.reshape(width, 3 * span), ffn_weight])
     next_out = lax.ppermute(
         w_out, "group", [(member, member - 1) for member in range(1, members)]
     )
@@ -294,12 +390,12 @@
         return matrix.reshape(length, local_heads, HEAD_DIM)
 
     stream = tokens[0].astype(jnp.float32)
+    unit_all = norm_forward(token_blocks.reshape(length, width).astype(jnp.float32))[1]
+    normed_attn = (unit_all * gains[0]).astype(low)
     saved_all = []
     outputs = []
     for layer in range(LAYERS):
         attn_weight, ffn_weight = weights[layer]
-        inverse_attn, unit_attn = norm_forward(stream)
-        normed_attn = gather((unit_attn * gains[layer]).astype(low), members)
         product = dot(normed_attn, attn_weight)
         queries = rotate(heads_of(product[:, :span]), cosine, sine_table).astype(low)
         keys = rotate(heads_of(product[:, span : 2 * span]), cosine, sine_table).astype(low)
@@ -312,46 +408,71 @@
         probs = (exponent / jnp.sum(exponent, axis=-1, keepdims=True)).astype(low)
         mixed = jnp.einsum("hts,shd->thd", probs, values, preferred_element_type=jnp.float32)
         mixed = mixed.reshape(length, span).astype(low)
-        after = stream + scatter_sum(dot(mixed, out_all[layer]), members)
-        inverse_ffn, unit_ffn = norm_forward(after)
-        normed_ffn = gather((unit_ffn * gains[LAYERS + layer]).astype(low), members)
+        after, normed_ffn = block_sum(
+            1, mixed, out_all[layer], stream, gains[LAYERS + layer], members
+        )
         both = dot(normed_ffn, ffn_weight)
         gate, up = both[:, :part_ff], both[:, part_ff:]
         hidden = (jax.nn.silu(gate) * up).astype(low)
-        stream = after + scatter_sum(dot(hidden, w_down[layer]), members)
+        saved_all.append(
+            (stream, normed_attn, queries, keys, values, probs, mixed, after, normed_ffn, gate, up, hidden)
+        )
+        if layer + 1 < LAYERS:
+            stream, normed_attn = block_sum(
+                2, hidden, w_down[layer], after, gains[layer + 1], members
+            )
+        else:
+            stream = block_sum(
+                3, hidden, w_down[layer], after, gains[layer], members, gathers=False
+            )[0]
         outputs.append(stream)
-        saved_all.append(
-            (
-                inverse_attn, unit_attn, normed_attn, queries, keys, values, probs, mixed,
-                inverse_ffn, unit_ffn, normed_ffn, gate, up, hidden,
-            )
-        )
+
+    def narrow(blocks):
+        wide = by_row(blocks)[:, : HEADS * HEAD_DIM].astype(jnp.float32)
+        wide = wide.reshape(own_rows, KV_HEADS, SHARE, HEAD_DIM)
+        return wide.sum(axis=2).reshape(own_rows, KV_HEADS * HEAD_DIM).astype(low)
 
     grad_result = cotangent[0].astype(jnp.float32)
-    owned = [None] * LAYERS
+    owned_attn = [None] * LAYERS
+    owned_ffn = [None] * LAYERS
     gain_sums = [None] * (2 * LAYERS)
+    previous = None
+
+    def replica_sum(shares, previous):
+        if previous is not None:
+            shares, previous = lax.optimization_barrier((shares, previous))
+        return lax.psum(shares, "replica"), previous
+
     for layer in reversed(range(LAYERS)):
         attn_weight, ffn_weight = weights[layer]
         (
-            inverse_attn, unit_attn, normed_attn, queries, keys, values, probs, mixed,
-            inverse_ffn, unit_ffn, normed_ffn, gate, up, hidden,
+            stream, normed_attn, queries, keys, values, probs, mixed, after, normed_ffn, gate, up, hidden
         ) = saved_all[layer]
-        out_low = gather(grad_result.astype(low), members)
         grad_hidden = against(out_low, w_down[layer])
         sigmoid = jax.nn.sigmoid(gate)
         grad_up = (grad_hidden * gate * sigmoid).astype(low)
         grad_gate = (grad_hidden * up * sigmoid * (1.0 + gate * (1.0 - sigmoid))).astype(low)
         grad_both = jnp.concatenate([grad_gate, grad_up], axis=1)
-        grad_normed_ffn = scatter_sum(against(grad_both, ffn_weight), members)
+        grad_after, gain_sums[LAYERS + layer], after_low = block_sum(
+            4, grad_both, ffn_weight.T, after, gains[LAYERS + layer], members, grad=grad_result
+        )
         grad_down = over_rows(hidden, out_low).astype(low)
         grad_ffn_weight = swap(
             over_rows(normed_ffn, grad_both).astype(low).reshape(members, own_rows, 2 * part_ff)
         )
-        gain_sums[LAYERS + layer] = jnp.sum(grad_normed_ffn * unit_ffn, axis=0)
-        grad_after = grad_result + norm_back(
-            grad_normed_ffn * gains[LAYERS + layer], unit_ffn, inverse_ffn
-        )
-        after_low = gather(grad_after.astype(low), members)
+        after_low, grad_ffn_weight, grad_down = lax.optimization_barrier(
+            (after_low, grad_ffn_weight, grad_down)
+        )
+        owned_ffn[layer], before = replica_sum(
+            (
+                by_row(grad_ffn_weight[:, :, :part_ff]),
+                by_row(grad_ffn_weight[:, :, part_ff:]),
+                grad_down,
+            ),
+            previous,
+        )
+        if before is not None:
+            owned_attn[layer + 1] = before
         grad_mixed = against(after_low, out_all[layer]).astype(low)
         grad_out = over_rows(mixed, after_low).astype(low)
         delta = jnp.sum(
@@ -379,15 +500,9 @@
             ],
             axis=1,
         ).astype(low)
-        grad_normed_attn = scatter_sum(against(back, attn_weight), members)
         grad_attn_weight = swap(
             over_rows(normed_attn, back).astype(low).reshape(members, own_rows, 3 * span)
         )
-        gain_sums[layer] = jnp.sum(grad_normed_attn * unit_attn, axis=0)
-        grad_result = grad_after + norm_back(
-            grad_normed_attn * gains[layer], unit_attn, inverse_attn
-        )
-
         before = lax.ppermute(
             grad_out, "group", [(member, member + 1) for member in range(members - 1)]
         )
@@ -397,29 +512,37 @@
             own_rows,
             0,
         )
-
-        def narrow(blocks):
-            wide = by_row(blocks)[:, : HEADS * HEAD_DIM].astype(jnp.float32)
-            wide = wide.reshape(own_rows, KV_HEADS, SHARE, HEAD_DIM)
-            return wide.sum(axis=2).reshape(own_rows, KV_HEADS * HEAD_DIM).astype(low)
-
-        shares = (
-            by_row(grad_attn_weight[:, :, :span])[:, : HEADS * HEAD_DIM],
-            narrow(grad_attn_weight[:, :, span : 2 * span]),
-            narrow(grad_attn_weight[:, :, 2 * span :]),
-            own_out,
-            by_row(grad_ffn_weight[:, :, :part_ff]),
-            by_row(grad_ffn_weight[:, :, part_ff:]),
-            grad_down,
-        )
-        if layer + 1 < LAYERS:
-            shares, owned[layer + 1] = lax.optimization_barrier((shares, owned[layer + 1]))
-        owned[layer] = lax.psum(shares, "replica")
-
-    gain_total = lax.psum(jnp.stack(gain_sums), ("group", "replica"))
+        if layer > 0:
+            grad_result, gain_sums[layer], out_low = block_sum(
+                5, back, attn_weight.T, stream, gains[layer], members, grad=grad_after
+            )
+            out_low, grad_attn_weight, own_out = lax.optimization_barrier(
+                (out_low, grad_attn_weight, own_out)
+            )
+        else:
+            grad_attn_weight, own_out, back = lax.optimization_barrier(
+                (grad_attn_weight, own_out, back)
+            )
+            grad_result, gain_sums[layer] = block_sum(
+                6, back, attn_weight.T, stream, gains[layer], members, grad=grad_after, gathers=False
+            )
+        previous, owned_ffn[layer] = replica_sum(
+            (
+                by_row(grad_attn_weight[:, :, :span])[:, : HEADS * HEAD_DIM],
+                narrow(grad_attn_weight[:, :, span : 2 * span]),
+                narrow(grad_attn_weight[:, :, 2 * span :]),
+                own_out,
+            ),
+            owned_ffn[layer],
+        )
+    owned_attn[0] = previous
+
+    gain_total = lax.psum(jnp.concatenate(gain_sums, axis=0), ("group", "replica"))
     gain_total = lax.dynamic_slice_in_dim(gain_total, owner * own_rows, own_rows, 1)
     stacked = [
-        jnp.stack([owned[layer][place] for layer in range(LAYERS)]).astype(jnp.float32)
+        jnp.stack([(owned_attn[layer] + owned_ffn[layer])[place] for layer in range(LAYERS)]).astype(
+            jnp.float32
+        )
         for place in range(7)
     ]
     return (

time: 743 us -> 722 us (0.972)
  waiting for transfers between devices: 125 us -> 89.4 us
  local copies, waits for them, and re-layouts: 82.4 us -> 115 us
  blocking collectives: 66.5 us -> 40.7 us
  other arithmetic: 38.7 us -> 52.1 us
  Pallas kernels: 267 us -> 280 us
  matrix products: 91.5 us -> 82.4 us
    all_gather x2 -> x0, blocking collectives: 25.2 us -> none  [the longest x1 15.8 us: on_device(): all_positions = lax.all_gather(positions[0], 'group', axis=0, tiled=True)]
    unnamed x260 -> x242, local copies, waits for them, and re-layouts: 30.3 us -> 52.8 us
    all_to_all x8 -> x7, waiting for transfers between devices: 21.3 us -> 2.73 us  [swap(): lax.all_to_all(blocks, 'group', split_axis=0, concat_axis=0, tiled=True)]
    convert_element_type x9 -> x4, local copies, waits for them, and re-layouts: 22.8 us -> 4.25 us  [the longest x2 2.88 us: on_device(): hidden = (jax.nn.silu(gate) * up).astype(low)]
    psum x2 -> x4, waiting for transfers between devices: 104 us -> 85.9 us  [replica_sum(): return (lax.psum(shares, 'replica'), previous)]
    pallas_call x16 -> x9, Pallas kernels: 267 us -> 280 us  [the longest x8 237 us: block_sum(): pl.pallas_call(lambda *refs: sum_kernel(members, backward, gathers, *refs...]
    reshape x0 -> x7, local copies, waits for them, and re-layouts: none -> 9.66 us  [the longest x2 4.54 us: on_device(): weights.append([attn_weight.reshape(width, 3 * span), ffn_weight])]
    dot_general x8 -> x4, matrix products: 20.9 us -> 12.8 us  [against(): lax.dot_general(left, right, (((1,), (1,)), ((), ())), preferred_element_...]
  transfers between devices with their start and end apart: 13 -> 15, of which waited for: 6 -> 4; matrix products, arithmetic and copies ran while one was open for 17% -> 26% of each run, Pallas kernels for 21% -> 39%
where the time goes in v2:
time: 722 us; the launch traced here: 716 us
  Pallas kernels  280 us (39%)
  local copies, waits for them, and re-layouts  115 us (16%)
  waiting for transfers between devices  89.4 us (12%)
  matrix products  82.4 us (11%)
  other arithmetic  52.1 us (7%)
  starting transfers between devices  41.5 us (6%)
  blocking collectives  40.7 us (6%)
  between operations  15.5 us (2%)
    pallas_call x8, Pallas kernels, block_sum(): pl.pallas_call(lambda *refs: sum_kernel(members, backward, gathers, *refs...  237 us
    psum x4, waiting for transfers between devices, replica_sum(): return (lax.psum(shares, 'replica'), previous)  85.9 us
    unnamed x242, local copies, waits for them, and re-layouts  52.8 us
    pallas_call x1, Pallas kernels, first_exchange(): pl.pallas_call(lambda *refs: first_kernel(members, *refs), out_shape=[jax...  42.7 us
    psum x1, blocking collectives, on_device(): lax.psum(jnp.concatenate(gain_sums, axis=0), ('group', 'replica'))  40.7 us
    all_to_all x7, starting transfers between devices, swap(): lax.all_to_all(blocks, 'group', split_axis=0, concat_axis=0, tiled=True)  33.1 us
    dot_general x8, matrix products, over_rows(): lax.dot_general(left, right, (((0,), (0,)), ((), ())), preferred_element_...  21.8 us
    sub x2, matrix products, on_device(): exponent = jnp.exp(scores - jnp.max(scores, axis=-1, keepdims=True))  16.2 us
  transfers between devices with their start and end apart: 15, of which 4 were waited for; matrix products, arithmetic and copies ran while one was open for 26% of the time, Pallas kernels for 39%

profile of v2, /device:TPU:0, one launch (start us, length us, event | category | flops | bytes accessed | tf_op | source)
XLA Modules:
  0.0 716.1 jit_solution(12031034536281749297)
XLA Ops:
  14.1 6.8 all-to-all-start
  23.7 42.7 %shard_map.203 = (bf16[8,128,960]{2,1,0:T(8,128)(2,1)S(1)}, f32[8,8,128]{2,1,0:T(8,128)S(1)}, bf16[8,120,384]{2,1,0:T(8,128)(2,1)S(1)}) custom-call(bf16[128,960]{1,0:T(8,128)(2,1)S(1)} %bitcast.309, f32[8,128]{1,0:T(8,128)S(1)} %select_maximum_fusion.refs_1_, bf16[8,120,384]{2,1,0:T(8,128)(2,1)S(1)} %pad_maximum_fusion.6.refs_2_), custom_call_target="tpu_custom_call" | custom-call | bytes 60000000 | tf_op jit(solution)/shard_map/pallas_call | solution.py:137
  83.5 8.1 %fusion.66 = (f32[2,1024]{1,0:T(2,128)S(1)}, f32[2,1024,1024]{1,2,0:T(8,128)}) fusion(pred[1024,1024]{0,1:T(8,128)(4,1)} %fusion.10, bf16[1024,2,32]{0,2,1:T(8,128)(2,1)} %get-tuple-element.230, bf16[1024,2,32]{0,2,1:T(8,128)(2,1)} %get-tuple-element.231, bf16[1024,2,32]{0,2,1:T(8,128)(2,1)} %get-tuple-element.211, bf16[1024,2,32]{0,2,1:T(8,128)(2,1)} %get-tuple-element.210), kind=kOutput, calls=%fused_computation.194 | convolution fusion | flops 277873664 | bytes 9969664 | tf_op jit(solution)/shard_map/sub | solution.py:407
  91.6 4.6 divide_convert_fusion.1
  114.9 32.0 %shard_map.204 = (f32[128,960]{1,0:T(8,128)S(1)}, bf16[8,128,960]{2,1,0:T(8,128)(2,1)S(1)}) custom-call(bf16[8,128,128]{2,1,0:T(8,128)(2,1)S(1)} %copy.187.refs_0_, bf16[128,960]{1,0:T(8,128)(2,1)S(1)} %get-tuple-element.221.refs_1_, f32[128,960]{1,0:T(8,128)S(1)} %get-tuple-element.256.refs_2_, f32[1,960]{1,0:T(1,128)S(1)} %slice.230.refs_3_), custom_call_target="tpu_custom_call" | custom-call | bytes 90000000 | tf_op jit(solution)/shard_map/pallas_call | solution.py:246
  164.0 33.1 %shard_map.205 = (f32[128,960]{1,0:T(8,128)S(1)}, bf16[8,128,960]{2,1,0:T(8,128)(2,1)S(1)}) custom-call(bf16[8,128,320]{2,1,0:T(8,128)(2,1)S(1)} %bitcast.308, bf16[320,960]{1,0:T(8,128)(2,1)S(1)} %copy-done.8, f32[128,960]{1,0:T(8,128)S(1)} %copy-done.19, f32[1,960]{1,0:T(1,128)S(1)} %slice.237.refs_3_), custom_call_target="tpu_custom_call" | custom-call | bytes 90000000 | tf_op jit(solution)/shard_map/pallas_call | solution.py:246
  198.4 4.5 all-to-all-start.2
  207.5 8.1 %fusion.67 = (f32[2,1024]{1,0:T(2,128)S(1)}, f32[2,1024,1024]{1,2,0:T(8,128)}) fusion(pred[1024,1024]{0,1:T(8,128)(4,1)} %fusion.10, bf16[1024,2,32]{0,2,1:T(8,128)(2,1)} %get-tuple-element.228, bf16[1024,2,32]{0,2,1:T(8,128)(2,1)} %get-tuple-element.229, bf16[1024,2,32]{0,2,1:T(8,128)(2,1)} %get-tuple-element.207, bf16[1024,2,32]{0,2,1:T(8,128)(2,1)} %get-tuple-element.206), kind=kOutput, calls=%fused_computation.195 | convolution fusion | flops 277873664 | bytes 9969664 | tf_op jit(solution)/shard_map/sub | solution.py:407
  215.6 4.6 divide_convert_fusion
  223.2 33.1 %shard_map.206 = (f32[128,960]{1,0:T(8,128)S(1)}, bf16[8,128,960]{2,1,0:T(8,128)(2,1)S(1)}) custom-call(bf16[8,128,128]{2,1,0:T(8,128)(2,1)S(1)} %copy.196.refs_0_, bf16[128,960]{1,0:T(8,128)(2,1)S(1)} %copy-done.21, f32[128,960]{1,0:T(8,128)S(1)} %get-tuple-element.69.refs_2_, f32[1,960]{1,0:T(1,128)S(1)} %slice.250.refs_3_), custom_call_target="tpu_custom_call" | custom-call | bytes 90000000 | tf_op jit(solution)/shard_map/pallas_call | solution.py:246
  258.5 5.1 fusion.71
  263.6 4.6 multiply_convert_fusion.6
  271.1 4.8 all-to-all-start.3
  286.8 33.3 %shard_map.208 = (f32[128,960]{1,0:T(8,128)S(1)}, f32[1,960]{1,0:T(1,128)S(1)}, bf16[8,128,960]{2,1,0:T(8,128)(2,1)S(1)}) custom-call(bf16[8,128,640]{2,1,0:T(8,128)(2,1)S(1)} %bitcast.301, bf16[640,960]{1,0:T(8,128)(2,1)S(1)} %bitcast.300, f32[128,960]{1,0:T(8,128)S(1)} %copy-done.13, f32[1,960]{1,0:T(1,128)S(1)} %slice.250.refs_3_, f32[128,960]{1,0:T(8,128)S(1)} %copy-done.17), custom_call_target="tpu_custom_call" | custom-call | bytes 90000000 | tf_op jit(solution)/shard_map/pallas_call | solution.py:246
  362.4 32.3 %shard_map.209 = (f32[128,960]{1,0:T(8,128)S(1)}, f32[1,960]{1,0:T(1,128)S(1)}, bf16[8,128,960]{2,1,0:T(8,128)(2,1)S(1)}) custom-call(bf16[8,128,384]{2,1,0:T(8,128)(2,1)S(1)} %pad_maximum_fusion.4.refs_0_, bf16[384,960]{1,0:T(8,128)(2,1)S(1)} %bitcast.307, f32[128,960]{1,0:T(8,128)S(1)} %copy-done.4, f32[1,960]{1,0:T(1,128)S(1)} %slice.237.refs_3_, ...), custom_call_target="tpu_custom_call" | custom-call | bytes 90000000 | tf_op jit(solution)/shard_map/pallas_call | solution.py:246
  405.7 4.3 all-to-all-start.5
  418.5 20.3 %shard_map.207 = f32[128,960]{1,0:T(8,128)S(1)} custom-call(bf16[8,128,320]{2,1,0:T(8,128)(2,1)S(1)} %bitcast.304, bf16[320,960]{1,0:T(8,128)(2,1)S(1)} %copy-done.7, f32[128,960]{1,0:T(8,128)S(1)} %copy-done.14, f32[1,960]{1,0:T(1,128)S(1)} %slice.237.refs_3_), custom_call_target="tpu_custom_call" | custom-call | bytes 90000000 | tf_op jit(solution)/shard_map/pallas_call | solution.py:246
  459.7 31.7 %shard_map.210 = (f32[128,960]{1,0:T(8,128)S(1)}, f32[1,960]{1,0:T(1,128)S(1)}, bf16[8,128,960]{2,1,0:T(8,128)(2,1)S(1)}) custom-call(bf16[8,128,640]{2,1,0:T(8,128)(2,1)S(1)} %bitcast.302, bf16[640,960]{1,0:T(8,128)(2,1)S(1)} %bitcast.299, f32[128,960]{1,0:T(8,128)S(1)} %copy-done.20, f32[1,960]{1,0:T(1,128)S(1)} %slice.230.refs_3_, f32[128,960]{1,0:T(8,128)S(1)} %copy-done.28), custom_call_target="tpu_custom_call" | custom-call | bytes 90000000 | tf_op jit(solution)/shard_map/pallas_call | solution.py:246
  509.6 18.2 %all-reduce.24.cloned.1.call-done = (bf16[120,2560]{0,1:T(8,128)(2,1)}, bf16[120,2560]{0,1:T(8,128)(2,1)}, bf16[320,960]{1,0:T(8,128)(2,1)}) async-done(((bf16[120,2560]{0,1:T(8,128)(2,1)}, bf16[120,2560]{0,1:T(8,128)(2,1)}, bf16[320,960]{1,0:T(8,128)(2,1)}), (bf16[120,2560]{0,1:T(8,128)(2,1)}, bf16[120,2560]{0,1:T(8,128)(2,1)}, bf16[320,960]{1,0:T(8,128)(2,1)})) %all-reduce.24.cloned.1.call-update) | async-done | bytes 1843216 | tf_op jit(solution)/shard_map/psum | solution.py:444
  534.4 36.5 %all-reduce.22.cloned.1.call-done = (bf16[120,960]{1,0:T(8,128)(2,1)}, bf16[120,320]{0,1:T(8,128)(2,1)}, bf16[120,320]{0,1:T(8,128)(2,1)}, bf16[120,960]{0,1:T(8,128)(2,1)}) async-done(((bf16[120,960]{1,0:T(8,128)(2,1)}, bf16[120,320]{0,1:T(8,128)(2,1)}, bf16[120,320]{0,1:T(8,128)(2,1)}, bf16[120,960]{0,1:T(8,128)(2,1)}), (bf16[120,960]{1,0:T(8,128)(2,1)}, bf16[120,320]{0,1:T(8,128)(2,1)}, ...) | async-done | bytes 614416 | tf_op jit(solution)/shard_map/psum | solution.py:444
  577.4 4.3 all-to-all-start.6
  599.4 21.3 %shard_map.211 = (f32[128,960]{1,0:T(8,128)S(1)}, f32[1,960]{1,0:T(1,128)S(1)}) custom-call(bf16[8,128,384]{2,1,0:T(8,128)(2,1)S(1)} %bitcast.306, bf16[384,960]{1,0:T(8,128)(2,1)S(1)} %bitcast.305, f32[128,960]{1,0:T(8,128)S(1)} %copy-done.2, f32[1,960]{1,0:T(1,128)S(1)} %slice.264.refs_3_, f32[128,960]{1,0:T(8,128)S(1)} %copy-done.24), custom_call_target="tpu_custom_call" | custom-call | bytes 90000000 | tf_op jit(solution)/shard_map/pallas_call | solution.py:246
  621.7 40.7 %psum.105 = f32[4,960]{1,0:T(4,128)S(1)} all-reduce(f32[4,960]{1,0:T(4,128)S(1)} %pad_maximum_fusion.38), channel_id=1, replica_groups=mesh['group'=8,'replica'=4] {'group','replica'}, use_global_device_ids=true, to_apply=%region_7.8 | all-reduce | flops 3840 | bytes 30720 | tf_op jit(solution)/shard_map/psum | solution.py:540
  673.1 31.2 %all-reduce.18.cloned.1.call-done = (bf16[1,120,960]{2,1,0:T(8,128)(2,1)}, bf16[1,120,320]{1,2,0:T(8,128)(2,1)}, bf16[1,120,320]{1,2,0:T(8,128)(2,1)}, bf16[1,120,960]{1,2,0:T(8,128)(2,1)}) async-done(((bf16[1,120,960]{2,1,0:T(8,128)(2,1)}, bf16[1,120,320]{1,2,0:T(8,128)(2,1)}, bf16[1,120,320]{1,2,0:T(8,128)(2,1)}, bf16[1,120,960]{1,2,0:T(8,128)(2,1)}), (bf16[1,120,960]{2,1,0:T(8,128)(2,1)}, ...) | async-done | bytes 614416 | tf_op jit(solution)/shard_map/psum | solution.py:444
  (410 shorter events, 234.4 us)
Async XLA Ops:
  7.2 105.5 %collective-permute-start = (bf16[2,120,960]{2,1,0:T(8,128)(2,1)}, bf16[2,120,960]{2,1,0:T(8,128)(2,1)}, u32[]{:S(2)}, u32[]{:S(2)}) collective-permute-start(bf16[2,120,960]{2,1,0:T(8,128)(2,1)} %param.18), channel_id=1, source_target_pairs={{4,0},{8,4},{12,8},{16,12},{20,16},{24,20},{28,24},{5,1},{9,5},{13... | collective-permute-start | bytes 1382408 | tf_op jit(solution)/shard_map/ppermute | solution.py:375
  14.1 135.8 %all-to-all-start = ((bf16[8,120,640]{2,1,0:T(8,128)(2,1)}), bf16[8,120,640]{2,1,0:T(8,128)(2,1)}, u32[]{:S(2)}, u32[]{:S(2)}) async-start(bf16[8,120,640]{2,1,0:T(8,128)(2,1)} %copy.190), calls=%async_computation | async-start | bytes 2457600 | tf_op jit(solution)/shard_map/all_to_all | solution.py:264
  20.9 242.7 %all-gather.3.cloned.1.call-start = ((), (), s32[]{:S(2)}) async-start(), calls=%async_computation.7 | async-start | bytes 2211840 | tf_op jit(solution)/shard_map/all_gather | solution.py:368
  72.7 23.6 %copy-start.41 = (bf16[1024,128]{0,1:T(8,128)(2,1)}, bf16[1024,128]{0,1:T(8,128)(2,1)S(1)}, u32[]{:S(2)}) copy-start(bf16[1024,128]{0,1:T(8,128)(2,1)S(1)} %slice.392) | copy-start | bytes 786436
  114.0 35.9 %copy-start.49 = (bf16[2,128,960]{2,1,0:T(8,128)(2,1)}, bf16[2,128,960]{2,1,0:T(8,128)(2,1)S(1)}, u32[]{:S(2)}) copy-start(bf16[2,128,960]{2,1,0:T(8,128)(2,1)S(1)} %fusion.34) | copy-start | bytes 1474564
  149.9 48.5 %all-to-all-start.1 = ((bf16[8,120,384]{2,1,0:T(8,128)(2,1)}), bf16[8,120,384]{2,1,0:T(8,128)(2,1)}, u32[]{:S(2)}, u32[]{:S(2)}) async-start(bf16[8,120,384]{2,1,0:T(8,128)(2,1)} %copy.194), calls=%async_computation.1 | async-start | bytes 1474560 | tf_op jit(solution)/shard_map/all_to_all | solution.py:264
  198.4 24.8 %copy-start.3 = (f32[128,960]{1,0:T(8,128)}, f32[128,960]{1,0:T(8,128)S(1)}, u32[]{:S(2)}) copy-start(f32[128,960]{1,0:T(8,128)S(1)} %get-tuple-element.69.refs_2_) | copy-start | bytes 1474564
  198.4 60.1 %all-to-all-start.2 = ((bf16[8,120,640]{2,1,0:T(8,128)(2,1)}), bf16[8,120,640]{2,1,0:T(8,128)(2,1)}, u32[]{:S(2)}, u32[]{:S(2)}) async-start(bf16[8,120,640]{2,1,0:T(8,128)(2,1)} %copy.199), calls=%async_computation.2 | async-start | bytes 2457600 | tf_op jit(solution)/shard_map/all_to_all | solution.py:264
  271.1 52.9 %all-to-all-start.3 = ((bf16[8,120,640]{2,1,0:T(8,128)(2,1)}), bf16[8,120,640]{2,1,0:T(8,128)(2,1)}, u32[]{:S(2)}, u32[]{:S(2)}) async-start(bf16[8,120,640]{2,1,0:T(8,128)(2,1)} %bitcast.63), calls=%async_computation.3 | async-start | bytes 2457600 | tf_op jit(solution)/shard_map/all_to_all | solution.py:264
  286.8 35.4 %copy-start.75 = (bf16[1024,320]{0,1:T(8,128)(2,1)S(1)}, bf16[1024,320]{0,1:T(8,128)(2,1)}, u32[]{:S(2)}) copy-start(bf16[1024,320]{0,1:T(8,128)(2,1)} %get-tuple-element.183) | copy-start | bytes 1966084
  286.8 35.4 %copy-start.109 = (bf16[1,1024,960]{1,2,0:T(8,128)(2,1)S(1)}, bf16[1,1024,960]{1,2,0:T(8,128)(2,1)}, u32[]{:S(2)}) copy-start(bf16[1,1024,960]{1,2,0:T(8,128)(2,1)} %all-gather.3.cloned.1.call-done) | copy-start | bytes 5898244
  339.1 59.7 %all-to-all-start.4 = ((bf16[8,120,384]{2,1,0:T(8,128)(2,1)}), bf16[8,120,384]{2,1,0:T(8,128)(2,1)}, u32[]{:S(2)}, u32[]{:S(2)}) async-start(bf16[8,120,384]{2,1,0:T(8,128)(2,1)} %bitcast.391), calls=%async_computation.4 | async-start | bytes 1474560 | tf_op jit(solution)/shard_map/all_to_all | solution.py:264
  346.5 50.4 %collective-permute-start.1 = (bf16[128,960]{0,1:T(8,128)(2,1)}, bf16[128,960]{0,1:T(8,128)(2,1)}, u32[]{:S(2)}, u32[]{:S(2)}) collective-permute-start(bf16[128,960]{0,1:T(8,128)(2,1)} %convolution_convert_fusion.12), channel_id=1, source_target_pairs={{0,4},{4,8},{8,12},{12,16},{16,20},{20,24},{24,28},{1,5},{5,9},{9,... | collective-permute-start | bytes 737288 | tf_op jit(solution)/shard_map/ppermute | solution.py:506
  405.7 87.8 %all-to-all-start.5 = ((bf16[8,120,640]{2,1,0:T(8,128)(2,1)}), bf16[8,120,640]{2,1,0:T(8,128)(2,1)}, u32[]{:S(2)}, u32[]{:S(2)}) async-start(bf16[8,120,640]{2,1,0:T(8,128)(2,1)} %bitcast.347), calls=%async_computation.5 | async-start | bytes 2457600 | tf_op jit(solution)/shard_map/all_to_all | solution.py:264
  410.0 117.9 %all-reduce.24.cloned.1.call-start = ((), (), s32[]{:S(2)}) async-start(), calls=%async_computation.11 | async-start | bytes 3932160 | tf_op jit(solution)/shard_map/psum | solution.py:444
  445.5 125.4 %all-reduce.22.cloned.1.call-start = ((), (), s32[]{:S(2)}) async-start(), calls=%async_computation.10 | async-start | bytes 1310720 | tf_op jit(solution)/shard_map/psum | solution.py:444
  527.9 135.1 %all-reduce.20.cloned.1.call-start = ((), (), s32[]{:S(2)}) async-start(), calls=%async_computation.9 | async-start | bytes 3932160 | tf_op jit(solution)/shard_map/psum | solution.py:444
  530.7 40.2 %copy-start.86 = (bf16[1024,2,32]{0,2,1:T(8,128)(2,1)S(1)}, bf16[1024,2,32]{0,2,1:T(8,128)(2,1)}, u32[]{:S(2)}) copy-start(bf16[1024,2,32]{0,2,1:T(8,128)(2,1)} %get-tuple-element.224) | copy-start | bytes 393220
  577.4 16.4 %all-to-all-start.6 = ((bf16[8,120,384]{2,1,0:T(8,128)(2,1)}), bf16[8,120,384]{2,1,0:T(8,128)(2,1)}, u32[]{:S(2)}, u32[]{:S(2)}) async-start(bf16[8,120,384]{2,1,0:T(8,128)(2,1)} %bitcast.392), calls=%async_computation.6 | async-start | bytes 1474560 | tf_op jit(solution)/shard_map/all_to_all | solution.py:264
  581.7 122.5 %all-reduce.18.cloned.1.call-start = ((), (), s32[]{:S(2)}) async-start(), calls=%async_computation.8 | async-start | bytes 1310720 | tf_op jit(solution)/shard_map/psum | solution.py:444
  583.7 5.5 collective-permute-start.2
  670.3 34.0 %copy-start.90 = (bf16[120,960]{0,1:T(8,128)(2,1)S(1)}, bf16[120,960]{0,1:T(8,128)(2,1)}, u32[]{:S(2)}) copy-start(bf16[120,960]{0,1:T(8,128)(2,1)} %get-tuple-element.110) | copy-start | bytes 691204
  673.1 33.6 %copy-start.95 = (bf16[120,320]{0,1:T(8,128)(2,1)S(1)}, bf16[120,320]{0,1:T(8,128)(2,1)}, u32[]{:S(2)}) copy-start(bf16[120,320]{0,1:T(8,128)(2,1)} %get-tuple-element.108) | copy-start | bytes 230404
  673.1 34.4 %copy-start.94 = (bf16[120,320]{0,1:T(8,128)(2,1)S(1)}, bf16[120,320]{0,1:T(8,128)(2,1)}, u32[]{:S(2)}) copy-start(bf16[120,320]{0,1:T(8,128)(2,1)} %get-tuple-element.106) | copy-start | bytes 230404
  (102 other events, 341.0 us)
Sparse Core Ops, SparseCore 0:
  23.6 42.9 all-gather.2
  445.6 82.1 all-reduce.23
  530.5 40.4 all-reduce.21
  573.9 82.8 all-reduce.19
  663.1 41.0 all-reduce.17

commit v3 on v2

--- a/solution.py
+++ b/solution.py
@@ -14,6 +14,7 @@
 epsilon = 1e-05
 rope_base = 100000.0
 low = jnp.bfloat16
+COST = 3_000_000
 
 
 def dot(left, right):
@@ -252,7 +253,7 @@
         compiler_params=pltpu.CompilerParams(
             collective_id=name, has_side_effects=True, vmem_limit_bytes=32 * 2**20
         ),
-        cost_estimate=pl.CostEstimate(flops=0, bytes_accessed=90_000_000, transcendentals=0),
+        cost_estimate=pl.CostEstimate(flops=0, bytes_accessed=COST, transcendentals=0),
     )(*operands)
     result = list(result)
     if gathers:
@@ -433,15 +434,14 @@
         return wide.sum(axis=2).reshape(own_rows, KV_HEADS * HEAD_DIM).astype(low)
 
     grad_result = cotangent[0].astype(jnp.float32)
-    owned_attn = [None] * LAYERS
-    owned_ffn = [None] * LAYERS
     gain_sums = [None] * (2 * LAYERS)
-    previous = None
-
-    def replica_sum(shares, previous):
-        if previous is not None:
-            shares, previous = lax.optimization_barrier((shares, previous))
-        return lax.psum(shares, "replica"), previous
+    attn_shares = ()
+    groups = []
+
+    def replica_sum(shares):
+        if groups:
+            shares, groups[-1] = lax.optimization_barrier((shares, groups[-1]))
+        groups.append(lax.psum(shares, "replica"))
 
     for layer in reversed(range(LAYERS)):
         attn_weight, ffn_weight = weights[layer]
@@ -453,6 +453,8 @@
         grad_up = (grad_hidden * gate * sigmoid).astype(low)
         grad_gate = (grad_hidden * up * sigmoid * (1.0 + gate * (1.0 - sigmoid))).astype(low)
         grad_both = jnp.concatenate([grad_gate, grad_up], axis=1)
+        if groups:
+            grad_both, groups[-1] = lax.optimization_barrier((grad_both, groups[-1]))
         grad_after, gain_sums[LAYERS + layer], after_low = block_sum(
             4, grad_both, ffn_weight.T, after, gains[LAYERS + layer], members, grad=grad_result
         )
@@ -460,19 +462,13 @@
         grad_ffn_weight = swap(
             over_rows(normed_ffn, grad_both).astype(low).reshape(members, own_rows, 2 * part_ff)
         )
-        after_low, grad_ffn_weight, grad_down = lax.optimization_barrier(
-            (after_low, grad_ffn_weight, grad_down)
-        )
-        owned_ffn[layer], before = replica_sum(
-            (
-                by_row(grad_ffn_weight[:, :, :part_ff]),
-                by_row(grad_ffn_weight[:, :, part_ff:]),
-                grad_down,
-            ),
-            previous,
-        )
-        if before is not None:
-            owned_attn[layer + 1] = before
+        shares = (
+            by_row(grad_ffn_weight[:, :, :part_ff]),
+            by_row(grad_ffn_weight[:, :, part_ff:]),
+            grad_down,
+        ) + attn_shares
+        after_low, shares = lax.optimization_barrier((after_low, shares))
+        replica_sum(shares)
         grad_mixed = against(after_low, out_all[layer]).astype(low)
         grad_out = over_rows(mixed, after_low).astype(low)
         delta = jnp.sum(
@@ -512,37 +508,37 @@
             own_rows,
             0,
         )
+        attn_shares = (
+            by_row(grad_attn_weight[:, :, :span])[:, : HEADS * HEAD_DIM],
+            narrow(grad_attn_weight[:, :, span : 2 * span]),
+            narrow(grad_attn_weight[:, :, 2 * span :]),
+            own_out,
+        )
+        if layer + 1 == LAYERS:
+            back, outputs[-1] = lax.optimization_barrier((back, outputs[-1]))
         if layer > 0:
             grad_result, gain_sums[layer], out_low = block_sum(
                 5, back, attn_weight.T, stream, gains[layer], members, grad=grad_after
             )
-            out_low, grad_attn_weight, own_out = lax.optimization_barrier(
-                (out_low, grad_attn_weight, own_out)
-            )
+            out_low, attn_shares = lax.optimization_barrier((out_low, attn_shares))
         else:
-            grad_attn_weight, own_out, back = lax.optimization_barrier(
-                (grad_attn_weight, own_out, back)
-            )
+            attn_shares, back = lax.optimization_barrier((attn_shares, back))
             grad_result, gain_sums[layer] = block_sum(
                 6, back, attn_weight.T, stream, gains[layer], members, grad=grad_after, gathers=False
             )
-        previous, owned_ffn[layer] = replica_sum(
-            (
-                by_row(grad_attn_weight[:, :, :span])[:, : HEADS * HEAD_DIM],
-                narrow(grad_attn_weight[:, :, span : 2 * span]),
-                narrow(grad_attn_weight[:, :, 2 * span :]),
-                own_out,
-            ),
-            owned_ffn[layer],
-        )
-    owned_attn[0] = previous
+            grad_result, attn_shares = lax.optimization_barrier((grad_result, attn_shares))
+            replica_sum(attn_shares)
+    owned = [None] * LAYERS
+    for layer in range(LAYERS):
+        place = LAYERS - 1 - layer
+        owned[layer] = groups[place + 1][-4:] + groups[place][:3]
+    if LAYERS > 1:
+        owned[0] = groups[LAYERS][:4] + groups[LAYERS - 1][:3]
 
     gain_total = lax.psum(jnp.concatenate(gain_sums, axis=0), ("group", "replica"))
     gain_total = lax.dynamic_slice_in_dim(gain_total, owner * own_rows, own_rows, 1)
     stacked = [
-        jnp.stack([(owned_attn[layer] + owned_ffn[layer])[place] for layer in range(LAYERS)]).astype(
-            jnp.float32
-        )
+        jnp.stack([owned[layer][place] for layer in range(LAYERS)]).astype(jnp.float32)
         for place in range(7)
     ]
     return (

time: 722 us -> 674 us (0.934)
  waiting for transfers between devices: 89.4 us -> 43.5 us
  local copies, waits for them, and re-layouts: 115 us -> 107 us
    psum x4 -> x3, waiting for transfers between devices: 85.9 us -> 40 us  [replica_sum(): groups.append(lax.psum(shares, 'replica'))]
    unnamed x242 -> x231, local copies, waits for them, and re-layouts: 52.8 us -> 48.4 us
  transfers between devices with their start and end apart: 15 -> 14, of which waited for: 4 -> 3; matrix products, arithmetic and copies ran while one was open for 26% -> 24% of each run, Pallas kernels for 39% -> 42%
where the time goes in v3:
time: 674 us; the launch traced here: 669 us
  Pallas kernels  278 us (41%)
  local copies, waits for them, and re-layouts  107 us (16%)
  matrix products  86.7 us (13%)
  other arithmetic  54 us (8%)
  waiting for transfers between devices  43.5 us (6%)
  blocking collectives  42.5 us (6%)
  starting transfers between devices  40.9 us (6%)
  between operations  15.4 us (2%)
    pallas_call x8, Pallas kernels, block_sum(): pl.pallas_call(lambda *refs: sum_kernel(members, backward, gathers, *refs...  236 us
    unnamed x231, local copies, waits for them, and re-layouts  48.4 us
    pallas_call x1, Pallas kernels, first_exchange(): pl.pallas_call(lambda *refs: first_kernel(members, *refs), out_shape=[jax...  42.7 us
    psum x1, blocking collectives, on_device(): lax.psum(jnp.concatenate(gain_sums, axis=0), ('group', 'replica'))  42.5 us
    psum x3, waiting for transfers between devices, replica_sum(): groups.append(lax.psum(shares, 'replica'))  40 us
    all_to_all x7, starting transfers between devices, swap(): lax.all_to_all(blocks, 'group', split_axis=0, concat_axis=0, tiled=True)  33 us
    dot_general x8, matrix products, over_rows(): lax.dot_general(left, right, (((0,), (0,)), ((), ())), preferred_element_...  25.2 us
    sub x2, matrix products, on_device(): exponent = jnp.exp(scores - jnp.max(scores, axis=-1, keepdims=True))  16.2 us
  transfers between devices with their start and end apart: 14, of which 3 were waited for; matrix products, arithmetic and copies ran while one was open for 24% of the time, Pallas kernels for 42%

profile of v3, /device:TPU:0, one launch (start us, length us, event | category | flops | bytes accessed | tf_op | source)
XLA Modules:
  0.0 668.9 jit_solution(13354923667632305215)
XLA Ops:
  14.1 6.8 %all-to-all-start = ((bf16[8,120,640]{2,1,0:T(8,128)(2,1)}), bf16[8,120,640]{2,1,0:T(8,128)(2,1)}, u32[]{:S(2)}, u32[]{:S(2)}) async-start(bf16[8,120,640]{2,1,0:T(8,128)(2,1)} %copy.190), calls=%async_computation | async-start | bytes 2457600 | tf_op jit(solution)/shard_map/all_to_all | solution.py:265
  23.7 42.7 %shard_map.203 = (bf16[8,128,960]{2,1,0:T(8,128)(2,1)S(1)}, f32[8,8,128]{2,1,0:T(8,128)S(1)}, bf16[8,120,384]{2,1,0:T(8,128)(2,1)S(1)}) custom-call(bf16[128,960]{1,0:T(8,128)(2,1)S(1)} %bitcast.297, f32[8,128]{1,0:T(8,128)S(1)} %select_maximum_fusion.refs_1_, bf16[8,120,384]{2,1,0:T(8,128)(2,1)S(1)} %pad_maximum_fusion.6.refs_2_), custom_call_target="tpu_custom_call" | custom-call | bytes 60000000 | tf_op jit(solution)/shard_map/pallas_call | solution.py:138
  83.5 8.1 %fusion.60 = (f32[2,1024]{1,0:T(2,128)S(1)}, f32[2,1024,1024]{1,2,0:T(8,128)}) fusion(pred[1024,1024]{0,1:T(8,128)(4,1)} %fusion.10, bf16[1024,2,32]{0,2,1:T(8,128)(2,1)} %get-tuple-element.272, bf16[1024,2,32]{0,2,1:T(8,128)(2,1)} %get-tuple-element.273, bf16[1024,2,32]{0,2,1:T(8,128)(2,1)} %get-tuple-element.253, bf16[1024,2,32]{0,2,1:T(8,128)(2,1)} %get-tuple-element.252), kind=kOutput, calls=%fused_computation.188 | convolution fusion | flops 277873664 | bytes 9969664 | tf_op jit(solution)/shard_map/sub | solution.py:408
  91.6 4.6 divide_convert_fusion.1
  114.8 32.0 %shard_map.204 = (f32[128,960]{1,0:T(8,128)S(1)}, bf16[8,128,960]{2,1,0:T(8,128)(2,1)S(1)}) custom-call(bf16[8,128,128]{2,1,0:T(8,128)(2,1)S(1)} %copy.187.refs_0_, bf16[128,960]{1,0:T(8,128)(2,1)S(1)} %get-tuple-element.263.refs_1_, f32[128,960]{1,0:T(8,128)S(1)} %get-tuple-element.298.refs_2_, f32[1,960]{1,0:T(1,128)S(1)} %slice.230.refs_3_), custom_call_target="tpu_custom_call" | custom-call | bytes 3000000 | tf_op jit(solution)/shard_map/pallas_call | solution.py:247
  163.8 33.1 %shard_map.205 = (f32[128,960]{1,0:T(8,128)S(1)}, bf16[8,128,960]{2,1,0:T(8,128)(2,1)S(1)}) custom-call(bf16[8,128,320]{2,1,0:T(8,128)(2,1)S(1)} %bitcast.296, bf16[320,960]{1,0:T(8,128)(2,1)S(1)} %copy-done.9, f32[128,960]{1,0:T(8,128)S(1)} %copy-done.20, f32[1,960]{1,0:T(1,128)S(1)} %slice.237.refs_3_), custom_call_target="tpu_custom_call" | custom-call | bytes 3000000 | tf_op jit(solution)/shard_map/pallas_call | solution.py:247
  198.2 4.5 all-to-all-start.2
  207.4 8.1 %fusion.61 = (f32[2,1024]{1,0:T(2,128)S(1)}, f32[2,1024,1024]{1,2,0:T(8,128)}) fusion(pred[1024,1024]{0,1:T(8,128)(4,1)} %fusion.10, bf16[1024,2,32]{0,2,1:T(8,128)(2,1)} %get-tuple-element.270, bf16[1024,2,32]{0,2,1:T(8,128)(2,1)} %get-tuple-element.271, bf16[1024,2,32]{0,2,1:T(8,128)(2,1)} %get-tuple-element.249, bf16[1024,2,32]{0,2,1:T(8,128)(2,1)} %get-tuple-element.248), kind=kOutput, calls=%fused_computation.189 | convolution fusion | flops 277873664 | bytes 9969664 | tf_op jit(solution)/shard_map/sub | solution.py:408
  215.4 4.6 divide_convert_fusion
  223.1 33.1 %shard_map.206 = (f32[128,960]{1,0:T(8,128)S(1)}, bf16[8,128,960]{2,1,0:T(8,128)(2,1)S(1)}) custom-call(bf16[8,128,128]{2,1,0:T(8,128)(2,1)S(1)} %copy.196.refs_0_, bf16[128,960]{1,0:T(8,128)(2,1)S(1)} %copy-done.22, f32[128,960]{1,0:T(8,128)S(1)} %get-tuple-element.90.refs_2_, f32[1,960]{1,0:T(1,128)S(1)} %slice.251.refs_3_), custom_call_target="tpu_custom_call" | custom-call | bytes 3000000 | tf_op jit(solution)/shard_map/pallas_call | solution.py:247
  258.3 5.1 fusion.65
  263.4 4.6 multiply_convert_fusion.7
  271.0 4.4 all-to-all-start.3
  286.7 33.2 %shard_map.207 = (f32[128,960]{1,0:T(8,128)S(1)}, f32[1,960]{1,0:T(1,128)S(1)}, bf16[8,128,960]{2,1,0:T(8,128)(2,1)S(1)}) custom-call(bf16[8,128,640]{2,1,0:T(8,128)(2,1)S(1)} %bitcast.288, bf16[640,960]{1,0:T(8,128)(2,1)S(1)} %bitcast.286, f32[128,960]{1,0:T(8,128)S(1)} %copy-done.16, f32[1,960]{1,0:T(1,128)S(1)} %slice.251.refs_3_, f32[128,960]{1,0:T(8,128)S(1)} %copy-done.18), custom_call_target="tpu_custom_call" | custom-call | bytes 3000000 | tf_op jit(solution)/shard_map/pallas_call | solution.py:247
  349.0 4.4 all-to-all-start.4
  366.6 17.3 %shard_map.208 = f32[128,960]{1,0:T(8,128)S(1)} custom-call(bf16[8,128,320]{2,1,0:T(8,128)(2,1)S(1)} %bitcast.291, bf16[320,960]{1,0:T(8,128)(2,1)S(1)} %copy-done.8, f32[128,960]{1,0:T(8,128)S(1)} %copy-done.17, f32[1,960]{1,0:T(1,128)S(1)} %slice.237.refs_3_), custom_call_target="tpu_custom_call" | custom-call | bytes 3000000 | tf_op jit(solution)/shard_map/pallas_call | solution.py:247
  385.3 32.5 %shard_map.209 = (f32[128,960]{1,0:T(8,128)S(1)}, f32[1,960]{1,0:T(1,128)S(1)}, bf16[8,128,960]{2,1,0:T(8,128)(2,1)S(1)}) custom-call(bf16[8,128,384]{2,1,0:T(8,128)(2,1)S(1)} %bitcast.295, bf16[384,960]{1,0:T(8,128)(2,1)S(1)} %bitcast.294, f32[128,960]{1,0:T(8,128)S(1)} %copy-done.4, f32[1,960]{1,0:T(1,128)S(1)} %slice.237.refs_3_, f32[128,960]{1,0:T(8,128)S(1)} %copy-done.27), custom_call_target="tpu_custom_call" | custom-call | bytes 3000000 | tf_op jit(solution)/shard_map/pallas_call | solution.py:247
  432.3 4.8 convolution_convert_fusion
  437.2 4.4 all-to-all-start.5
  454.8 33.2 %shard_map.210 = (f32[128,960]{1,0:T(8,128)S(1)}, f32[1,960]{1,0:T(1,128)S(1)}, bf16[8,128,960]{2,1,0:T(8,128)(2,1)S(1)}) custom-call(bf16[8,128,640]{2,1,0:T(8,128)(2,1)S(1)} %bitcast.289, bf16[640,960]{1,0:T(8,128)(2,1)S(1)} %bitcast.287, f32[128,960]{1,0:T(8,128)S(1)} %copy-done.21, f32[1,960]{1,0:T(1,128)S(1)} %slice.230.refs_3_, f32[128,960]{1,0:T(8,128)S(1)} %copy-done.29), custom_call_target="tpu_custom_call" | custom-call | bytes 3000000 | tf_op jit(solution)/shard_map/pallas_call | solution.py:247
  541.5 21.3 %shard_map.211 = (f32[128,960]{1,0:T(8,128)S(1)}, f32[1,960]{1,0:T(1,128)S(1)}) custom-call(bf16[8,128,384]{2,1,0:T(8,128)(2,1)S(1)} %bitcast.293, bf16[384,960]{1,0:T(8,128)(2,1)S(1)} %bitcast.292, f32[128,960]{1,0:T(8,128)S(1)} %copy-done.2, f32[1,960]{1,0:T(1,128)S(1)} %slice.280.refs_3_, f32[128,960]{1,0:T(8,128)S(1)} %copy-done.25), custom_call_target="tpu_custom_call" | custom-call | bytes 3000000 | tf_op jit(solution)/shard_map/pallas_call | solution.py:247
  563.8 42.5 %psum.108 = f32[4,960]{1,0:T(4,128)S(1)} all-reduce(f32[4,960]{1,0:T(4,128)S(1)} %pad_maximum_fusion.40), channel_id=1, replica_groups=mesh['group'=8,'replica'=4] {'group','replica'}, use_global_device_ids=true, to_apply=%region_14.15 | all-reduce | flops 3840 | bytes 30720 | tf_op jit(solution)/shard_map/psum | solution.py:538
  607.0 6.7 %all-reduce.18.cloned.1.call-done = (bf16[120,2560]{0,1:T(8,128)(2,1)}, bf16[120,2560]{0,1:T(8,128)(2,1)}, bf16[320,960]{1,0:T(8,128)(2,1)}, bf16[120,960]{1,0:T...) async-done(((bf16[120,2560]{0,1:T(8,128)(2,1)}, bf16[120,2560]{0,1:T(8,128)(2,1)}, bf16[320,960]{1,0:T(8,128)(2,1)}, ...) | async-done | bytes 2457616 | tf_op jit(solution)/shard_map/psum | solution.py:444
  623.8 33.2 %all-reduce.16.cloned.1.call-done = (bf16[1,120,960]{2,1,0:T(8,128)(2,1)}, bf16[1,120,320]{1,2,0:T(8,128)(2,1)}, bf16[1,120,320]{1,2,0:T(8,128)(2,1)}, bf16[1,120,960]{1,2,0:T(8,128)(2,1)}) async-done(((bf16[1,120,960]{2,1,0:T(8,128)(2,1)}, bf16[1,120,320]{1,2,0:T(8,128)(2,1)}, bf16[1,120,320]{1,2,0:T(8,128)(2,1)}, bf16[1,120,960]{1,2,0:T(8,128)(2,1)}), (bf16[1,120,960]{2,1,0:T(8,128)(2,1)}, ...) | async-done | bytes 614416 | tf_op jit(solution)/shard_map/psum | solution.py:444
  (396 shorter events, 228.2 us)
Async XLA Ops:
  7.2 105.4 %collective-permute-start = (bf16[2,120,960]{2,1,0:T(8,128)(2,1)}, bf16[2,120,960]{2,1,0:T(8,128)(2,1)}, u32[]{:S(2)}, u32[]{:S(2)}) collective-permute-start(bf16[2,120,960]{2,1,0:T(8,128)(2,1)} %param.18), channel_id=1, source_target_pairs={{4,0},{8,4},{12,8},{16,12},{20,16},{24,20},{28,24},{5,1},{9,5},{13... | collective-permute-start | bytes 1382408 | tf_op jit(solution)/shard_map/ppermute | solution.py:376
  14.1 135.7 %all-to-all-start = ((bf16[8,120,640]{2,1,0:T(8,128)(2,1)}), bf16[8,120,640]{2,1,0:T(8,128)(2,1)}, u32[]{:S(2)}, u32[]{:S(2)}) async-start(bf16[8,120,640]{2,1,0:T(8,128)(2,1)} %copy.190), calls=%async_computation | async-start | bytes 2457600 | tf_op jit(solution)/shard_map/all_to_all | solution.py:265
  20.9 242.5 %all-gather.3.cloned.1.call-start = ((), (), s32[]{:S(2)}) async-start(), calls=%async_computation.7 | async-start | bytes 2211840 | tf_op jit(solution)/shard_map/all_gather | solution.py:369
  72.7 23.5 %copy-start.40 = (bf16[1024,128]{0,1:T(8,128)(2,1)}, bf16[1024,128]{0,1:T(8,128)(2,1)S(1)}, u32[]{:S(2)}) copy-start(bf16[1024,128]{0,1:T(8,128)(2,1)S(1)} %slice.402) | copy-start | bytes 786436
  113.9 35.8 %copy-start.48 = (bf16[2,128,960]{2,1,0:T(8,128)(2,1)}, bf16[2,128,960]{2,1,0:T(8,128)(2,1)S(1)}, u32[]{:S(2)}) copy-start(bf16[2,128,960]{2,1,0:T(8,128)(2,1)S(1)} %fusion.29) | copy-start | bytes 1474564
  149.8 48.5 %all-to-all-start.1 = ((bf16[8,120,384]{2,1,0:T(8,128)(2,1)}), bf16[8,120,384]{2,1,0:T(8,128)(2,1)}, u32[]{:S(2)}, u32[]{:S(2)}) async-start(bf16[8,120,384]{2,1,0:T(8,128)(2,1)} %copy.194), calls=%async_computation.1 | async-start | bytes 1474560 | tf_op jit(solution)/shard_map/all_to_all | solution.py:265
  198.2 24.8 %copy-start.3 = (f32[128,960]{1,0:T(8,128)}, f32[128,960]{1,0:T(8,128)S(1)}, u32[]{:S(2)}) copy-start(f32[128,960]{1,0:T(8,128)S(1)} %get-tuple-element.90.refs_2_) | copy-start | bytes 1474564
  198.2 60.1 %all-to-all-start.2 = ((bf16[8,120,640]{2,1,0:T(8,128)(2,1)}), bf16[8,120,640]{2,1,0:T(8,128)(2,1)}, u32[]{:S(2)}, u32[]{:S(2)}) async-start(bf16[8,120,640]{2,1,0:T(8,128)(2,1)} %copy.199), calls=%async_computation.2 | async-start | bytes 2457600 | tf_op jit(solution)/shard_map/all_to_all | solution.py:265
  271.0 52.8 %all-to-all-start.3 = ((bf16[8,120,640]{2,1,0:T(8,128)(2,1)}), bf16[8,120,640]{2,1,0:T(8,128)(2,1)}, u32[]{:S(2)}, u32[]{:S(2)}) async-start(bf16[8,120,640]{2,1,0:T(8,128)(2,1)} %bitcast.58), calls=%async_computation.3 | async-start | bytes 2457600 | tf_op jit(solution)/shard_map/all_to_all | solution.py:265
  275.4 156.9 %all-reduce.20.cloned.1.call-start = ((), (), s32[]{:S(2)}) async-start(), calls=%async_computation.10 | async-start | bytes 3932160 | tf_op jit(solution)/shard_map/psum | solution.py:444
  286.7 35.3 %copy-start.71 = (bf16[1024,320]{0,1:T(8,128)(2,1)S(1)}, bf16[1024,320]{0,1:T(8,128)(2,1)}, u32[]{:S(2)}) copy-start(bf16[1024,320]{0,1:T(8,128)(2,1)} %get-tuple-element.225) | copy-start | bytes 1966084
  286.7 35.3 %copy-start.105 = (bf16[1,1024,960]{1,2,0:T(8,128)(2,1)S(1)}, bf16[1,1024,960]{1,2,0:T(8,128)(2,1)}, u32[]{:S(2)}) copy-start(bf16[1,1024,960]{1,2,0:T(8,128)(2,1)} %all-gather.3.cloned.1.call-done) | copy-start | bytes 5898244
  349.0 72.8 %all-to-all-start.4 = ((bf16[8,120,384]{2,1,0:T(8,128)(2,1)}), bf16[8,120,384]{2,1,0:T(8,128)(2,1)}, u32[]{:S(2)}, u32[]{:S(2)}) async-start(bf16[8,120,384]{2,1,0:T(8,128)(2,1)} %bitcast.373), calls=%async_computation.4 | async-start | bytes 1474560 | tf_op jit(solution)/shard_map/all_to_all | solution.py:265
  356.7 63.2 %collective-permute-start.1 = (bf16[128,960]{0,1:T(8,128)(2,1)}, bf16[128,960]{0,1:T(8,128)(2,1)}, u32[]{:S(2)}, u32[]{:S(2)}) collective-permute-start(bf16[128,960]{0,1:T(8,128)(2,1)} %convolution_convert_fusion.12), channel_id=1, source_target_pairs={{0,4},{4,8},{8,12},{12,16},{16,20},{20,24},{24,28},{1,5},{5,9},{9,... | collective-permute-start | bytes 737288 | tf_op jit(solution)/shard_map/ppermute | solution.py:502
  363.2 22.0 %copy-start.4 = (f32[128,960]{1,0:T(8,128)S(1)}, f32[128,960]{1,0:T(8,128)}, u32[]{:S(2)}) copy-start(f32[128,960]{1,0:T(8,128)} %copy-done.3) | copy-start | bytes 1474564
  383.9 33.9 %copy-start.13 = (f32[128,960]{1,0:T(8,128)}, f32[128,960]{1,0:T(8,128)S(1)}, u32[]{:S(2)}) copy-start(f32[128,960]{1,0:T(8,128)S(1)} %shard_map.208) | copy-start | bytes 1474564
  437.2 52.9 %all-to-all-start.5 = ((bf16[8,120,640]{2,1,0:T(8,128)(2,1)}), bf16[8,120,640]{2,1,0:T(8,128)(2,1)}, u32[]{:S(2)}, u32[]{:S(2)}) async-start(bf16[8,120,640]{2,1,0:T(8,128)(2,1)} %bitcast.335), calls=%async_computation.5 | async-start | bytes 2457600 | tf_op jit(solution)/shard_map/all_to_all | solution.py:265
  441.6 172.1 %all-reduce.18.cloned.1.call-start = ((), (), s32[]{:S(2)}) async-start(), calls=%async_computation.9 | async-start | bytes 5242880 | tf_op jit(solution)/shard_map/psum | solution.py:444
  519.6 16.4 %all-to-all-start.6 = ((bf16[8,120,384]{2,1,0:T(8,128)(2,1)}), bf16[8,120,384]{2,1,0:T(8,128)(2,1)}, u32[]{:S(2)}, u32[]{:S(2)}) async-start(bf16[8,120,384]{2,1,0:T(8,128)(2,1)} %bitcast.374), calls=%async_computation.6 | async-start | bytes 1474560 | tf_op jit(solution)/shard_map/all_to_all | solution.py:265
  523.9 133.1 %all-reduce.16.cloned.1.call-start = ((), (), s32[]{:S(2)}) async-start(), calls=%async_computation.8 | async-start | bytes 1310720 | tf_op jit(solution)/shard_map/psum | solution.py:444
  525.6 5.8 collective-permute-start.2
  621.0 36.1 %copy-start.86 = (bf16[120,960]{0,1:T(8,128)(2,1)S(1)}, bf16[120,960]{0,1:T(8,128)(2,1)}, u32[]{:S(2)}) copy-start(bf16[120,960]{0,1:T(8,128)(2,1)} %get-tuple-element.152) | copy-start | bytes 691204
  623.8 35.7 %copy-start.91 = (bf16[120,320]{0,1:T(8,128)(2,1)S(1)}, bf16[120,320]{0,1:T(8,128)(2,1)}, u32[]{:S(2)}) copy-start(bf16[120,320]{0,1:T(8,128)(2,1)} %get-tuple-element.150) | copy-start | bytes 230404
  623.8 36.5 %copy-start.90 = (bf16[120,320]{0,1:T(8,128)(2,1)S(1)}, bf16[120,320]{0,1:T(8,128)(2,1)}, u32[]{:S(2)}) copy-start(bf16[120,320]{0,1:T(8,128)(2,1)} %get-tuple-element.148) | copy-start | bytes 230404
  (97 other events, 369.2 us)
Sparse Core Ops, SparseCore 0:
  23.6 42.9 all-gather.2
  345.4 82.7 all-reduce.19
  506.3 107.3 all-reduce.17
  616.7 40.2 all-reduce.15
